TPU v7x, 256 devices: a whole 4x4x8 slice. The times are simulated.
256 devices in a mesh: band: 128 (over z, y, x_hi, core), col: 2 (over x_lo).
Axes of the slice: x: 4 (x_hi: 2, x_lo: 2; x = x_hi * 2 + x_lo), y: 4, z: 8, core: 2. Of those that a mesh axis runs over, the one named last changes fastest.
Arguments:
- image: bfloat16 [512, 128, 512], P('band'), may hold values from -60 to 60
- timestep: int32 [1], replicated, may hold values from 0 to 999
- class_label: int32 [1], replicated, may hold values from 0 to 999
- class_table: bfloat16 [1000, 256], replicated, may hold values from -6 to 6
- fine_modulation: bfloat16 [256, 512], replicated, may hold values from -0.1875 to 0.1875
- coarse_modulation: bfloat16 [256, 1024], P(None, 'col'), may hold values from -0.1875 to 0.1875
- fine_project: bfloat16 [512, 1536], P(None, 'col'), may hold values from -0.25 to 0.25
- fine_output: bfloat16 [512, 512], P('col'), may hold values from -0.25 to 0.25
- fine_scales: float32 [8], replicated, may hold values from 4 to 12
- merge_weight: bfloat16 [8192, 1024], P(None, 'col'), may hold values from -0.0625 to 0.0625
- coarse_project: bfloat16 [1024, 3072], P('col', 'band'), may hold values from -0.1875 to 0.1875
- coarse_scales: float32 [16], replicated, may hold values from 8 to 16
Outputs:
- fine_mixed: bfloat16 [512, 128, 512], P('band', None, 'col')
- coarse_values: bfloat16 [128, 32, 1024], P('band', None, 'col')
All inputs are finite; a program needn't handle non-finite values.
Results may differ from a plain program's by a relative error of at most 0.04.
Values may be sent and summed in bfloat16 or wider, within the bound.
A program may use at most 64 MiB of HBM per device.

v0:
```python
import math

import jax
import jax.numpy as jnp
from jax import lax
from jax.sharding import PartitionSpec as P

HD = 64
KW = 7
MERGE = 4


EPSILON = 1e-06


def extended_2(cells, sides, width):
    for axis, dim in sides:
        count = lax.axis_size(axis)
        ends = count - 1
        head = lax.slice_in_dim(cells, 0, width, axis=dim)
        tail = lax.slice_in_dim(cells, cells.shape[dim] - width, cells.shape[dim], axis=dim)
        cells = jnp.concatenate(
            [
                lax.ppermute(tail, axis, [(i, (i + 1) % count) for i in range(ends)]),
                cells,
                lax.ppermute(head, axis, [((i + 1) % count, i) for i in range(ends)]),
            ],
            axis=dim,
        )
    return cells


def time_features(timestep, feature_count):
    half_width = feature_count // 2
    frequency = jnp.exp(-math.log(10000.0) * jnp.arange(half_width, dtype=jnp.float32) / half_width)
    angles = timestep.astype(jnp.float32) * frequency
    return jnp.concatenate([jnp.cos(angles), jnp.sin(angles)])


def unit_rows(values):
    scaled_rows = values * lax.rsqrt(jnp.mean(values * values, axis=-1, keepdims=True) + EPSILON)
    return (scaled_rows * (1.0 / math.sqrt(values.shape[-1]))).astype(jnp.bfloat16)


def global_attend(coarse_queries, coarse_keys, head_values, head_scale):
    key_count = coarse_keys.shape[0]
    block_size = math.gcd(key_count, 4096)
    block_count = key_count // block_size
    query_count = coarse_queries.shape[0]

    def attend(totals, key_pack):
        key_block, value_block = key_pack
        block_logits = head_scale * jnp.dot(
            coarse_queries, key_block.T, preferred_element_type=jnp.float32
        )
        block_weights = jnp.exp(block_logits)
        new_numer = totals[0] + jnp.dot(
            block_weights.astype(jnp.bfloat16), value_block, preferred_element_type=jnp.float32
        )
        new_denom = totals[1] + jnp.sum(block_weights, axis=-1)
        return ((new_numer, new_denom), None)

    start_totals = (
        jnp.zeros((query_count, HD), jnp.float32),
        jnp.zeros((query_count,), jnp.float32),
    )
    (head_numer, head_denom), _ = lax.scan(
        attend,
        start_totals,
        (
            coarse_keys.reshape(block_count, block_size, HD),
            head_values.reshape(block_count, block_size, HD),
        ),
    )
    return (head_numer / head_denom[:, None]).astype(jnp.bfloat16)


def shards(
    image,
    timestep,
    class_label,
    class_table,
    fine_modulation,
    coarse_modulation,
    fine_project,
    fine_output,
    fine_scales,
    merge_weight,
    coarse_project,
    coarse_scales,
):
    band_count = lax.axis_size("band")
    columns = lax.axis_size("col")
    band_index = lax.axis_index("band")
    col_index = lax.axis_index("col")
    local_rows, fine_width, model_width = image.shape
    heads_local = fine_project.shape[1] // (3 * HD)
    grid_height = local_rows * band_count
    catalog = jnp.arange(class_table.shape[0], dtype=jnp.int32)
    one_hot = (catalog == class_label[0]).astype(jnp.bfloat16)
    condition = jnp.dot(one_hot[None, :], class_table, preferred_element_type=jnp.float32)[
        0
    ] + time_features(timestep[0], class_table.shape[1])
    fine_gain = 1.0 + jnp.dot(
        condition, fine_modulation.astype(jnp.float32), precision=lax.Precision.HIGHEST
    )
    coarse_gain = 1.0 + jnp.dot(
        condition, coarse_modulation.astype(jnp.float32), precision=lax.Precision.HIGHEST
    )
    pixels = image.astype(jnp.float32)
    normed = (
        pixels * lax.rsqrt(jnp.mean(pixels * pixels, axis=-1, keepdims=True) + EPSILON) * fine_gain
    ).astype(jnp.bfloat16)
    project = jnp.dot(
        normed.reshape(-1, model_width), fine_project, preferred_element_type=jnp.float32
    ).astype(jnp.bfloat16)
    project = project.reshape(local_rows, fine_width, heads_local, 3, HD)
    queries = unit_rows(project[:, :, :, 0, :].astype(jnp.float32)).astype(jnp.float32)
    keyval = project[:, :, :, 1:, :].reshape(local_rows, fine_width, heads_local * 2 * HD)
    radius = KW // 2
    extended = extended_2(keyval, (("band", 0),), radius)
    extended = jnp.pad(extended, ((0, 0), (radius, radius), (0, 0)))
    extended = extended.reshape(
        local_rows + 2 * radius, fine_width + 2 * radius, heads_local, 2, HD
    )
    keys_pad = unit_rows(extended[:, :, :, 0, :].astype(jnp.float32))
    values_pad = extended[:, :, :, 1, :]
    scales_local = lax.dynamic_slice_in_dim(fine_scales, col_index * heads_local, heads_local)
    row_ids = band_index * local_rows + jnp.arange(local_rows, dtype=jnp.int32)[:, None]
    col_ids = jnp.arange(fine_width, dtype=jnp.int32)[None, :]
    numerator = jnp.zeros((local_rows, fine_width, heads_local, HD), jnp.float32)
    denominator = jnp.zeros((local_rows, fine_width, heads_local), jnp.float32)
    for row_off in range(-radius, radius + 1):
        for col_off in range(-radius, radius + 1):
            key_win = keys_pad[
                radius + row_off : radius + row_off + local_rows,
                radius + col_off : radius + col_off + fine_width,
            ].astype(jnp.float32)
            val_win = values_pad[
                radius + row_off : radius + row_off + local_rows,
                radius + col_off : radius + col_off + fine_width,
            ].astype(jnp.float32)
            inside = (
                (row_ids + row_off >= 0)
                & (row_ids + row_off < grid_height)
                & (col_ids + col_off >= 0)
                & (col_ids + col_off < fine_width)
            ).astype(jnp.float32)
            logits = scales_local * jnp.sum(queries * key_win, axis=-1)
            weight = jnp.exp(logits) * inside[:, :, None]
            numerator = numerator + weight[:, :, :, None] * val_win
            denominator = denominator + weight
    attended = (
        (numerator / denominator[:, :, :, None]).astype(jnp.bfloat16).reshape(-1, heads_local * HD)
    )
    branch = lax.psum(jnp.dot(attended, fine_output, preferred_element_type=jnp.float32), "col")
    fine_full = (
        (pixels.reshape(-1, model_width) + branch)
        .astype(jnp.bfloat16)
        .reshape(local_rows, fine_width, model_width)
    )
    half_width = model_width // columns
    fine_mixed = lax.dynamic_slice_in_dim(fine_full, col_index * half_width, half_width, 2)
    coarse_cols = fine_width // MERGE
    patches = (
        fine_full.reshape(MERGE, coarse_cols, MERGE, model_width)
        .transpose(1, 0, 2, 3)
        .reshape(coarse_cols, MERGE * MERGE * model_width)
    )
    merged = jnp.dot(patches, merge_weight, preferred_element_type=jnp.float32).astype(jnp.bfloat16)
    merged_wide = merged.astype(jnp.float32)
    feature_half = merged.shape[1]
    coarse_width = feature_half * columns
    heads_half = coarse_width // HD // columns
    groups = band_count // heads_half
    query_width = coarse_cols // groups
    scaled = (merged_wide * coarse_gain).astype(jnp.bfloat16)
    partial_value = jnp.dot(
        scaled,
        lax.all_gather(coarse_project, "band", axis=1, tiled=True),
        preferred_element_type=jnp.float32,
    )
    squares = jnp.broadcast_to(
        jnp.sum(merged_wide * merged_wide, axis=-1, keepdims=True), (coarse_cols, columns)
    )
    summed, square_sum = (
        lax.psum_scatter(partial_value, "col", scatter_dimension=1, tiled=True),
        lax.psum_scatter(squares, "col", scatter_dimension=1, tiled=True),
    )
    factor = lax.rsqrt(square_sum[:, 0] / coarse_width + EPSILON)
    coarse_qkv = (
        (factor[:, None] * summed).astype(jnp.bfloat16).reshape(coarse_cols, heads_half, 3, HD)
    )
    query_part = coarse_qkv[:, :, 0, :].reshape(groups, query_width, heads_half, HD)
    keyval_part = (
        coarse_qkv[:, :, 1:, :].reshape(coarse_cols, heads_half, 2 * HD).transpose(1, 0, 2)
    )
    query_send = query_part.transpose(2, 0, 1, 3).reshape(band_count, query_width * HD)
    keyval_send = jnp.broadcast_to(
        keyval_part[:, None], (heads_half, groups, coarse_cols, 2 * HD)
    ).reshape(band_count, coarse_cols, 2 * HD)
    head_slot = band_index // groups
    query_got, keyval_got = (
        lax.all_to_all(query_send, "band", split_axis=0, concat_axis=0, tiled=True),
        lax.all_to_all(keyval_send, "band", split_axis=0, concat_axis=0, tiled=True),
    )
    coarse_queries = unit_rows(query_got.reshape(-1, HD).astype(jnp.float32))
    keyval_flat = keyval_got.reshape(-1, 2 * HD)
    coarse_keys = unit_rows(keyval_flat[:, :HD].astype(jnp.float32))
    head_values = keyval_flat[:, HD:]
    head_index = col_index * heads_half + head_slot
    head_scale = lax.dynamic_slice_in_dim(coarse_scales, head_index, 1)[0]
    head_out = global_attend(coarse_queries, coarse_keys, head_values, head_scale).reshape(
        band_count, query_width * HD
    )
    returned = lax.all_to_all(head_out, "band", split_axis=0, concat_axis=0, tiled=True)
    arranged = returned.reshape(heads_half, groups, query_width, HD).transpose(1, 2, 0, 3)
    coarse_values = arranged.reshape(1, coarse_cols, heads_half * HD)
    return (fine_mixed, coarse_values)


def solution(mesh):
    in_specs = (
        P("band", None, None),
        P(),
        P(),
        P(),
        P(),
        P(None, "col"),
        P(None, "col"),
        P("col", None),
        P(),
        P(None, "col"),
        P("col", "band"),
        P(),
    )
    out_specs = (P("band", None, "col"), P("band", None, "col"))
    return jax.shard_map(shards, mesh=mesh, in_specs=in_specs, out_specs=out_specs, check_vma=False)
```

profile of v0, /device:TPU:1, one launch (start us, length us, event | category | flops | bytes accessed | tf_op | source)
XLA Modules:
  0.0 305.8 jit_solution(3618576152108284730)
XLA Ops:
  9.5 1.2 fusion.106
  10.7 1.2 fusion.107
  11.9 1.2 multiply_reduce_fusion
  13.1 1.2 multiply_convert_fusion
  14.4 0.6 convolution_convert_fusion
  15.4 0.5 fusion.104
  16.0 5.2 %collective-permute-start.1 = (bf16[3,128,512]{1,2,0:T(8,128)(2,1)S(1)}, bf16[3,128,512]{1,2,0:T(8,128)(2,1)}, u32[]{:S(2)}, u32[]{:S(2)}) collective-permute-start(bf16[3,128,512]{1,2,0:T(8,128)(2,1)S(1)} %bitcast.179), channel_id=1, source_target_pairs={{2,0},{4,2},{6,4},{8,6},{10,8},{12,10},{14,12},{16,14},{18,16},{20... | collective-permute-start | bytes 1179656 | tf_op jit(solution)/shard_map/ppermute | solution.py:26
  21.3 2.8 collective-permute-start
  25.0 2.6 collective-permute-done.1
  27.6 5.4 %collective-permute-done = bf16[3,128,512]{1,2,0:T(8,128)(2,1)} collective-permute-done((bf16[3,128,512]{1,2,0:T(8,128)(2,1)S(1)}, bf16[3,128,512]{1,2,0:T(8,128)(2,1)}, u32[]{:S(2)}, u32[]{:S(2)}) %collective-permute-start) | collective-permute-done | bytes 393248 | tf_op jit(solution)/shard_map/ppermute | solution.py:24
  33.0 2.7 fusion.9
  36.0 0.9 fusion.2
  37.0 1.2 fusion.4
  38.1 2.6 fusion.32
  40.7 2.5 fusion.31
  43.2 2.8 fusion.33
  45.9 2.8 fusion.34
  48.7 3.8 %fusion.36 = (f32[4,128,4]{1,0,2:T(4,128)S(1)}, f32[4,128,4]{1,0,2:T(4,128)S(1)}, f32[4,128,4]{1,0,2:T(4,128)S(1)}, f32[4,128,4]{1,0,2:T(4,128)S(1)}, f32[4,128,...) fusion(bf16[10,134,4,64]{1,0,3,2:T(8,128)(2,1)S(1)} %fusion.4, ...), kind=kLoop, calls=%fused_computation.96 | loop fusion | flops 5740544 | bytes 3784704 | tf_op jit(solution)/shard_map/reduce_sum | solution.py:149
  52.5 0.5 add_add_fusion
  53.6 4.6 %divide_convert_fusion = bf16[4,128,4,64]{1,3,2,0:T(8,128)(2,1)S(1)} fusion(bf16[10,134,4,64]{1,3,2,0:T(8,128)(2,1)S(1)} %get-tuple-element.132, f32[4,128,4]{1,2,0:T(4,128)S(1)} %copy.225, f32[4,128,4]{1,2,0:T(4,128)S(1)} %copy.224, f32[4,128,4]{1,2,0:T(4,128)S(1)} %copy.223, f32[4,128,4]{1,2,0:T(4,128)S(1)} %copy.222, f32[4,128,4]{1,2,0:T(4,128)S(1)} %copy.221, ...), kind=kLoop, calls=%fused_computation.141 | loop fusion | flops 19398656 | bytes 13516800 | tf_op jit(solution)/shard_map/convert_element_type | solution.py:154
  58.5 1.3 fusion.80
  59.9 0.5 all-gather.2.cloned.1.call-update
  60.7 54.3 %all-reduce.4.cloned.1.call-done = f32[512,512]{1,0:T(8,128)} async-done(((f32[512,512]{1,0:T(8,128)}), f32[512,512]{1,0:T(8,128)}) %all-reduce.4.cloned.1.call-update) | async-done | bytes 1048592 | tf_op jit(solution)/shard_map/psum | solution.py:156
  115.1 1.4 fusion.24
  116.9 0.4 reshape.2597
  117.3 5.0 %multiply_reduce_fusion.2 = (f32[32]{0:T(128)S(1)}, f32[32,512]{1,0:T(8,128)S(1)}) fusion(bf16[32,8192]{1,0:T(8,128)(2,1)S(1)} %reshape.2597, bf16[8192,512]{1,0:T(8,128)(2,1)} %param.21), kind=kOutput, calls=%fused_computation.153 | convolution fusion | flops 268500960 | bytes 8978560 | tf_op jit(solution)/shard_map/dot_general | solution.py:170
  122.3 66.8 %all-gather.2.cloned.1.call-done = bf16[512,3072]{0,1:T(8,128)(2,1)} async-done(((bf16[512,24]{0,1:T(8,128)(2,1)}), bf16[512,3072]{0,1:T(8,128)(2,1)}) %all-gather.2.cloned.1.call-update) | async-done | bytes 3145744 | tf_op jit(solution)/shard_map/all_gather | solution.py:180
  189.1 3.7 %fusion.85 = f32[32,3072]{1,0:T(8,128)} fusion(bf16[512,3072]{0,1:T(8,128)(2,1)} %all-gather.2.cloned.1.call-done, f32[32,512]{1,0:T(8,128)S(1)} %get-tuple-element.290, f32[512]{0:T(512)S(1)} %broadcast_add_fusion), kind=kOutput, calls=%fused_computation.155 | convolution fusion | flops 100696064 | bytes 3606528 | tf_op jit(solution)/shard_map/dot_general | solution.py:178
  192.8 0.6 dynamic-slice.2
  193.4 3.8 %all-reduce.1 = f32[32,2]{0,1:T(2,128)S(1)} all-reduce(f32[32,2]{0,1:T(2,128)S(1)} %broadcast_in_dim.4), channel_id=2, replica_groups=mesh['band'=128,'col'=2] {'col'}, use_global_device_ids=true, to_apply=%region_54.55.clone | all-reduce | flops 64 | bytes 512
  197.2 0.7 rsqrt_bitcast_fusion
  197.8 9.6 %reduce-scatter.2.cloned.1.call-done = f32[32,1536]{1,0:T(8,128)} async-done(((f32[32,3072]{1,0:T(8,128)}), f32[32,1536]{1,0:T(8,128)}) %reduce-scatter.2.cloned.1.call-update) | async-done | bytes 196624 | tf_op jit(solution)/shard_map/reduce_scatter | solution.py:187
  207.4 1.0 multiply_convert_fusion.1
  208.8 0.7 all_to_all.20
  209.5 13.6 %all-to-all-start = ((bf16[128,1,128]{2,1,0:T(2,128)(2,1)}), bf16[128,1,128]{2,1,0:T(2,128)(2,1)S(1)}, u32[]{:S(2)}, u32[]{:S(2)}) async-start(bf16[128,1,128]{2,1,0:T(2,128)(2,1)} %all_to_all.20), calls=%async_computation.1 | async-start | bytes 131072 | tf_op jit(solution)/shard_map/all_to_all | solution.py:204
  223.4 11.4 %all-to-all-done = bf16[128,1,128]{2,1,0:T(2,128)(2,1)S(1)} async-done(((bf16[128,1,128]{2,1,0:T(2,128)(2,1)}), bf16[128,1,128]{2,1,0:T(2,128)(2,1)S(1)}, u32[]{:S(2)}, u32[]{:S(2)}) %all-to-all-start) | async-done | bytes 32800 | tf_op jit(solution)/shard_map/all_to_all | solution.py:204
  234.8 1.1 broadcast_in_dim.5
  236.0 6.3 %all-to-all-start.1 = ((bf16[128,32,128]{2,1,0:T(8,128)(2,1)}), bf16[128,32,128]{2,1,0:T(8,128)(2,1)S(1)}, u32[]{:S(2)}, u32[]{:S(2)}) async-start(bf16[128,32,128]{2,1,0:T(8,128)(2,1)} %bitcast.24), calls=%async_computation.2 | async-start | bytes 2097152 | tf_op jit(solution)/shard_map/all_to_all | solution.py:205
  242.3 0.6 dynamic_slice.16
  243.3 29.8 %all-to-all-done.1 = bf16[128,32,128]{2,1,0:T(8,128)(2,1)S(1)} async-done(((bf16[128,32,128]{2,1,0:T(8,128)(2,1)}), bf16[128,32,128]{2,1,0:T(8,128)(2,1)S(1)}, u32[]{:S(2)}, u32[]{:S(2)}) %all-to-all-start.1) | async-done | bytes 1048608 | tf_op jit(solution)/shard_map/all_to_all | solution.py:205
  273.0 0.6 fusion.10
  273.7 2.2 fusion.105
  275.9 1.3 fusion.18
  277.4 0.7 all_to_all.21
  278.1 7.4 %all-to-all-start.2 = ((bf16[128,1,128]{2,1,0:T(2,128)(2,1)}), bf16[128,1,128]{2,1,0:T(2,128)(2,1)S(1)}, u32[]{:S(2)}, u32[]{:S(2)}) async-start(bf16[128,1,128]{2,1,0:T(2,128)(2,1)} %all_to_all.21), calls=%async_computation.3 | async-start | bytes 131072 | tf_op jit(solution)/shard_map/all_to_all | solution.py:216
  285.5 0.7 constant_dynamic-slice_fusion
  286.2 11.1 %all-to-all-done.2 = bf16[128,1,128]{2,1,0:T(2,128)(2,1)S(1)} async-done(((bf16[128,1,128]{2,1,0:T(2,128)(2,1)}), bf16[128,1,128]{2,1,0:T(2,128)(2,1)S(1)}, u32[]{:S(2)}, u32[]{:S(2)}) %all-to-all-start.2) | async-done | bytes 32800 | tf_op jit(solution)/shard_map/all_to_all | solution.py:216
  297.6 0.7 reshape.2603
  (121 shorter events, 4.4 us)
Async XLA Ops:
  8.0 6.4 %copy-start = (bf16[512,768]{1,0:T(8,128)(2,1)S(1)}, bf16[512,768]{1,0:T(8,128)(2,1)}, u32[]{:S(2)}) copy-start(bf16[512,768]{1,0:T(8,128)(2,1)} %param.18) | copy-start | bytes 2359300
  8.0 107.1 %all-reduce.4.cloned.1.call-start = ((), (), s32[]{:S(2)}) async-start(), calls=%async_computation.4 | async-start | bytes 2097152 | tf_op jit(solution)/shard_map/psum | solution.py:156
  15.9 8.9 %copy-start.4 = (f32[8]{0:T(128)S(1)}, f32[8]{0:T(128)}, u32[]{:S(2)}) copy-start(f32[8]{0:T(128)} %param.20) | copy-start | bytes 100
  16.0 11.6 %collective-permute-start.1 = (bf16[3,128,512]{1,2,0:T(8,128)(2,1)S(1)}, bf16[3,128,512]{1,2,0:T(8,128)(2,1)}, u32[]{:S(2)}, u32[]{:S(2)}) collective-permute-start(bf16[3,128,512]{1,2,0:T(8,128)(2,1)S(1)} %bitcast.179), channel_id=1, source_target_pairs={{2,0},{4,2},{6,4},{8,6},{10,8},{12,10},{14,12},{16,14},{18,16},{20... | collective-permute-start | bytes 1179656 | tf_op jit(solution)/shard_map/ppermute | solution.py:26
  21.3 11.7 %collective-permute-start = (bf16[3,128,512]{1,2,0:T(8,128)(2,1)S(1)}, bf16[3,128,512]{1,2,0:T(8,128)(2,1)}, u32[]{:S(2)}, u32[]{:S(2)}) collective-permute-start(bf16[3,128,512]{1,2,0:T(8,128)(2,1)S(1)} %bitcast.180), channel_id=1, source_target_pairs={{0,2},{2,4},{4,6},{6,8},{8,10},{10,12},{12,14},{14,16},{16,18},{18... | collective-permute-start | bytes 1179656 | tf_op jit(solution)/shard_map/ppermute | solution.py:24
  53.6 4.9 %copy-start.3 = (bf16[256,512]{1,0:T(8,128)(2,1)S(1)}, bf16[256,512]{1,0:T(8,128)(2,1)}, u32[]{:S(2)}) copy-start(bf16[256,512]{1,0:T(8,128)(2,1)} %param.19) | copy-start | bytes 786436
  58.3 2.2 copy-start.2
  58.3 56.8 %copy-start.1 = (bf16[4,128,512]{2,1,0:T(8,128)(2,1)S(1)}, bf16[4,128,512]{2,1,0:T(8,128)(2,1)}, u32[]{:S(2)}) copy-start(bf16[4,128,512]{2,1,0:T(8,128)(2,1)} %param.12) | copy-start | bytes 1572868
  59.9 129.3 %all-gather.2.cloned.1.call-start = ((), (), s32[]{:S(2)}) async-start(), calls=%async_computation.5 | async-start | bytes 3170304 | tf_op jit(solution)/shard_map/all_gather | solution.py:180
  60.4 147.0 %reduce-scatter.2.cloned.1.call-start = ((), (), s32[]{:S(2)}) async-start(), calls=%async_computation.6 | async-start | bytes 589824 | tf_op jit(solution)/shard_map/reduce_scatter | solution.py:187
  122.3 70.5 %copy-start.6 = (u32[256]{0:T(256)S(1)}, u32[256]{0:T(256)}, u32[]{:S(2)}) copy-start(u32[256]{0:T(256)} %constant.110) | copy-start | bytes 3076
  197.8 44.4 %copy-start.5 = (f32[16]{0:T(128)S(1)}, f32[16]{0:T(128)}, u32[]{:S(2)}) copy-start(f32[16]{0:T(128)} %param.23) | copy-start | bytes 196
  209.5 25.3 %all-to-all-start = ((bf16[128,1,128]{2,1,0:T(2,128)(2,1)}), bf16[128,1,128]{2,1,0:T(2,128)(2,1)S(1)}, u32[]{:S(2)}, u32[]{:S(2)}) async-start(bf16[128,1,128]{2,1,0:T(2,128)(2,1)} %all_to_all.20), calls=%async_computation.1 | async-start | bytes 131072 | tf_op jit(solution)/shard_map/all_to_all | solution.py:204
  236.0 37.1 %all-to-all-start.1 = ((bf16[128,32,128]{2,1,0:T(8,128)(2,1)}), bf16[128,32,128]{2,1,0:T(8,128)(2,1)S(1)}, u32[]{:S(2)}, u32[]{:S(2)}) async-start(bf16[128,32,128]{2,1,0:T(8,128)(2,1)} %bitcast.24), calls=%async_computation.2 | async-start | bytes 2097152 | tf_op jit(solution)/shard_map/all_to_all | solution.py:205
  278.1 19.2 %all-to-all-start.2 = ((bf16[128,1,128]{2,1,0:T(2,128)(2,1)}), bf16[128,1,128]{2,1,0:T(2,128)(2,1)S(1)}, u32[]{:S(2)}, u32[]{:S(2)}) async-start(bf16[128,1,128]{2,1,0:T(2,128)(2,1)} %all_to_all.21), calls=%async_computation.3 | async-start | bytes 131072 | tf_op jit(solution)/shard_map/all_to_all | solution.py:216
Sparse Core Ops, SparseCore 0:
  60.0 55.0 all-reduce.3
  192.9 14.4 reduce-scatter.1
Sparse Core Ops, SparseCore 1:
  64.9 124.2 all-gather.1
where the time goes:
time: 306 us
  waiting for transfers between devices  192 us (63%)
  starting transfers between devices  35.3 us (12%)
  other arithmetic  31.5 us (10%)
  between operations  17.8 us (6%)
  matrix products  16.7 us (5%)
  local copies, waits for them, and re-layouts  9.12 us (3%)
  blocking collectives  3.77 us (1%)
    all_gather x1, waiting for transfers between devices, shards(): lax.all_gather(coarse_project, 'band', axis=1, tiled=True)  66.8 us
    psum x1, waiting for transfers between devices, shards(): lax.psum(jnp.dot(attended, fine_output, preferred_element_type=jnp.float3...  54.3 us
    all_to_all x1, waiting for transfers between devices, shards(): lax.all_to_all(keyval_send, 'band', split_axis=0, concat_axis=0, tiled=True)  29.8 us
    reduce_sum x5, other arithmetic, shards(): logits = scales_local * jnp.sum(queries * key_win, axis=-1)  14.4 us
    all_to_all x1, starting transfers between devices, shards(): lax.all_to_all(query_send, 'band', split_axis=0, concat_axis=0, tiled=True)  13.6 us
    all_to_all x1, waiting for transfers between devices, shards(): lax.all_to_all(query_send, 'band', split_axis=0, concat_axis=0, tiled=True)  11.4 us
    all_to_all x1, waiting for transfers between devices, shards(): lax.all_to_all(head_out, 'band', split_axis=0, concat_axis=0, tiled=True)  11.1 us
    reduce_scatter x1, waiting for transfers between devices, shards(): lax.psum_scatter(partial_value, 'col', scatter_dimension=1, tiled=True)  9.57 us
  transfers between devices with their start and end apart: 8, of which 8 were waited for; matrix products, arithmetic and copies ran while one was open for 4% of the time, Pallas kernels for 0%

commit v1 on v0

v1 whole, which is shorter than its diff:
```python
import math

import jax
import jax.numpy as jnp
from jax import lax
from jax.experimental import pallas as pl
from jax.experimental.pallas import tpu as pltpu
from jax.sharding import PartitionSpec as P

EPSILON = 1e-06
LOG2E = math.log2(math.e)
BF = jnp.bfloat16
F32 = jnp.float32
MESH = pl.DeviceIdType.MESH
BANDS = 128


def dot(a, b):
    return jnp.dot(a, b, preferred_element_type=F32)


def dot_t(a, b):
    return lax.dot_general(a, b, (((1,), (1,)), ((), ())), preferred_element_type=F32)


def iota(shape, dim):
    return lax.broadcasted_iota(jnp.int32, shape, dim)


def kernel(
    timestep,
    label,
    fine_scales,
    coarse_scales,
    image,
    class_table,
    fine_modulation,
    coarse_modulation,
    fine_project,
    fine_output,
    merge_weight,
    coarse_project,
    fine_out,
    coarse_out,
    xb,
    table_v,
    fmod_v,
    cmod_v,
    fproj_v,
    wperm,
    fout_v,
    merge_v,
    cproj_v,
    qs,
    kb,
    vb,
    att_own,
    att_got,
    fine_v,
    macc,
    mg,
    gb,
    gain_v,
    wb,
    kvs,
    qsend,
    kvb,
    qb,
    num,
    den,
    ob,
    rb,
    cv_v,
    load_sem,
    merge_sem,
    halo_send,
    halo_recv,
    pair_send,
    pair_recv,
    att_send,
    att_recv,
    fine_sem,
    w_send,
    w_recv,
    g_send,
    g_recv,
    kv_send,
    kv_recv,
    q_send,
    q_recv,
    fw_send,
    fw_recv,
    r_send,
    r_recv,
):
    band = lax.axis_index("band")
    c = lax.axis_index("col")
    core = lax.rem(band, 2)
    xh = lax.rem(lax.div(band, 2), 2)
    y = lax.rem(lax.div(band, 4), 4)
    z = lax.div(band, 16)
    x = 2 * xh + c

    def dev(zz, yy, xx, kk):
        return (((zz * 4 + yy) * 2 + lax.div(xx, 2)) * 2 + kk, lax.rem(xx, 2))

    sibling = dev(z, y, x, 1 - core)
    partner = (band, 1 - c)
    slow = (lax.rem(band + BANDS - 1 + 2 * core, BANDS), 1 - c)

    def row_of(u):
        return u + (1 - core) * (3 - 2 * u)

    def load(src, dst, k):
        return pltpu.make_async_copy(src, dst, load_sem.at[k])

    loads = [
        load(fine_modulation, fmod_v, 4),
        load(class_table, table_v, 5),
        load(fine_project, fproj_v, 6),
        load(coarse_modulation, cmod_v, 7),
        load(coarse_project, cproj_v, 8),
        load(fine_output, fout_v.at[c], 9),
    ]
    rows = [load(image.at[row_of(u)], xb.at[3 + u], u) for u in range(4)]
    merges = [
        pltpu.make_async_copy(merge_weight.at[row_of(u)], merge_v.at[u], merge_sem.at[u])
        for u in range(4)
    ]
    for copy in loads[:3]:
        copy.start()
    for copy in rows:
        copy.start()
    for copy in loads[3:]:
        copy.start()

    barrier = pltpu.get_barrier_semaphore()

    def signal(device):
        pl.semaphore_signal(barrier, inc=1, device_id=device, device_id_type=MESH)

    signal(slow)
    signal(sibling)

    def signal_line(k, carry):
        signal(dev(lax.rem(z + lax.div(k, 4), 8), y, lax.rem(x + lax.rem(k, 4), 4), core))
        return carry

    def signal_plane(k, carry):
        signal(dev(z, lax.rem(y + lax.div(k, 4), 4), lax.rem(x + lax.rem(k, 4), 4), core))
        return carry

    lax.fori_loop(1, 32, signal_line, 0)
    lax.fori_loop(4, 16, signal_plane, 0)
    pl.semaphore_wait(barrier, 45)

    def remote(src, dst, send, recv, device):
        return pltpu.make_async_remote_copy(
            src_ref=src,
            dst_ref=dst,
            send_sem=send,
            recv_sem=recv,
            device_id=device,
            device_id_type=MESH,
        )

    slow_copies = [
        remote(
            image.at[row_of(3 - j)], xb.at[7 + j], halo_send.at[j], halo_recv.at[j], slow
        )
        for j in range(3)
    ]
    fast_copies = [
        remote(
            image.at[row_of(j)], xb.at[2 - j], halo_send.at[3 + j], halo_recv.at[3 + j], sibling
        )
        for j in range(3)
    ]
    for copy in slow_copies + fast_copies:
        copy.start()
    fout_copy = remote(fine_output, fout_v.at[c], pair_send.at[0], pair_recv.at[0], partner)
    fout_copy.start()
    for copy in merges:
        copy.start()

    loads[4].wait()
    eye = (iota((32, 24), 0) == iota((32, 24), 1)).astype(BF)
    wb[core, y, x] = dot_t(eye, cproj_v[...]).astype(BF)

    def w_line(k):
        return remote(
            wb.at[core, y, x],
            wb.at[core, y, x],
            w_send.at[k],
            w_recv.at[k],
            dev(z, y, lax.rem(x + k, 4), core),
        )

    def w_plane(k):
        return remote(
            wb.at[core, y],
            wb.at[core, y],
            w_send.at[3 + k],
            w_recv.at[3 + k],
            dev(z, lax.rem(y + k, 4), x, core),
        )

    w_core = remote(wb.at[core], wb.at[core], w_send.at[0], w_recv.at[0], sibling)
    for k in (1, 2, 3):
        w_line(k).start()

    lane = iota((8, 256), 1)
    freq = jnp.exp((-math.log(10000.0) / 128.0) * lax.rem(lane, 128).astype(F32))
    angle = timestep[0].astype(F32) * freq
    time = jnp.where(lane < 128, jnp.cos(angle), jnp.sin(angle))
    one_hot = (iota((8, 1000), 1) == label[0]).astype(F32).astype(BF)
    loads[1].wait()
    condition = dot(one_hot, table_v[...]) + time
    c_hi = condition.astype(BF)
    rest = condition - c_hi.astype(F32)
    c_mid = rest.astype(BF)
    c_lo = (rest - c_mid.astype(F32)).astype(BF)

    def gain_of(weights):
        return 1.0 + (dot(c_hi, weights) + (dot(c_mid, weights) + dot(c_lo, weights)))

    loads[0].wait()
    fine_gain = gain_of(fmod_v[...])[0:1, :]
    loads[3].wait()
    gain_v[c] = gain_of(cmod_v[...])
    gain_copy = remote(gain_v.at[c], gain_v.at[c], pair_send.at[1], pair_recv.at[1], partner)
    gain_copy.start()

    loads[2].wait()
    fp = fproj_v[...]
    for part in range(3):
        for h in range(4):
            wperm[:, 256 * part + 64 * h : 256 * part + 64 * h + 64] = fp[
                :, 192 * h + 64 * part : 192 * h + 64 * part + 64
            ]
    ones_block = (lax.div(iota((256, 256), 0), 64) == lax.div(iota((256, 256), 1), 64)).astype(
        F32
    ).astype(BF)
    lane_head = lax.div(iota((1, 256), 1), 64)
    q_scale = jnp.zeros((1, 256), F32)
    for h in range(4):
        q_scale = jnp.where(lane_head == h, fine_scales[4 * c + h] * (LOG2E / 8.0), q_scale)

    def unit_factor(u):
        sq = u * u
        hi = sq.astype(BF)
        lo = (sq - hi.astype(F32)).astype(BF)
        return lax.rsqrt((dot(hi, ones_block) + dot(lo, ones_block)) * (1.0 / 64.0) + EPSILON)

    def normed_of(pixels):
        wide = pixels.astype(F32)
        mean = jnp.mean(wide * wide, axis=-1, keepdims=True)
        return (wide * lax.rsqrt(mean + EPSILON) * fine_gain).astype(BF)

    def keys_values(normed):
        kv = dot(normed, wperm[:, 256:768]).astype(BF)
        key = kv[:, :256].astype(F32)
        return (key * unit_factor(key) * 0.125).astype(BF), kv[:, 256:]

    for copy in rows:
        copy.wait()
    normed = normed_of(xb[3:7].reshape(512, 512))
    key, value = keys_values(normed)
    kb[3:7] = key.reshape(4, 128, 256)
    vb[3:7] = value.reshape(4, 128, 256)
    query = dot(normed, wperm[:, 0:256]).astype(BF).astype(F32)
    query = query * unit_factor(query) * q_scale
    for h in range(4):
        qs[:, 128 * h : 128 * h + 128, :] = (
            jnp.where(lane_head == h, query, 0.0).astype(BF).reshape(4, 128, 256)
        )
    for copy in fast_copies:
        copy.wait_recv()
    key, value = keys_values(normed_of(xb[0:3].reshape(384, 512)))
    kb[0:3] = key.reshape(3, 128, 256)
    vb[0:3] = value.reshape(3, 128, 256)

    distance = iota((128, 128), 0) - iota((128, 128), 1)
    far = jnp.where((distance <= 3) & (distance >= -3), 0.0, -1e30)
    macc[...] = jnp.zeros_like(macc)
    perm = (iota((128, 128), 1) == 4 * lax.rem(iota((128, 128), 0), 32) + lax.div(iota((128, 128), 0), 32)).astype(F32).astype(BF)

    def att_copy(r):
        return remote(att_own.at[r], att_got.at[r], att_send.at[r], att_recv.at[r], partner)

    def fine_copy(r):
        return pltpu.make_async_copy(fine_v.at[r], fine_out.at[row_of(r)], fine_sem.at[r])

    def attend_row(r):
        keys = kb[pl.ds(r, 7)].reshape(896, 256)
        values = vb[pl.ds(r, 7)].reshape(896, 256)
        bias = []
        for d in range(7):
            row = 4 * band + row_of(r + d - 3)
            outside = jnp.where((row < 0) | (row >= 4 * BANDS), -1e30, 0.0)
            bias.append(far + outside)
        bias = jnp.concatenate(bias, axis=1)
        logits = dot_t(qs[r], keys).reshape(4, 128, 896) + bias[None]
        weight = jnp.exp2(logits)
        total = jnp.sum(weight, axis=-1, keepdims=True)
        out = dot(weight.astype(BF).reshape(512, 896), values).reshape(4, 128, 256) * (1.0 / total)
        mixed = jnp.zeros((128, 256), F32)
        for h in range(4):
            mixed = jnp.where(lane_head == h, out[h], mixed)
        att_own[r] = mixed.astype(BF)
        att_copy(r).start()

    def mix_row(r):
        att_copy(r).wait_recv()
        merge_copy = pltpu.make_async_copy(
            merge_weight.at[row_of(r)], merge_v.at[r], merge_sem.at[r]
        )
        merge_copy.wait()
        full = (
            xb[3 + r].astype(F32) + dot(att_own[r], fout_v[c]) + dot(att_got[r], fout_v[1 - c])
        )
        fine_v[r] = jnp.where(c == 0, full[:, :256], full[:, 256:]).astype(BF)
        fine_copy(r).start()
        patches = dot(perm, full.astype(BF)).astype(BF)
        part = macc[...]
        for p in range(4):
            part = part + dot(patches[32 * p : 32 * p + 32], merge_v[r, 512 * p : 512 * p + 512, :])
        macc[...] = part

    def row_step(r, carry):
        @pl.when((r >= 1) & (r < 4))
        def _():
            slow_copy = remote(
                image.at[row_of(4 - r)],
                xb.at[6 + r],
                halo_send.at[r - 1],
                halo_recv.at[r - 1],
                slow,
            )
            slow_copy.wait_recv()
            key, value = keys_values(normed_of(xb[6 + r]))
            kb[6 + r] = key
            vb[6 + r] = value

        @pl.when(r < 4)
        def _():
            attend_row(r)

        @pl.when(r == 1)
        def _():
            for k in (1, 2, 3):
                w_line(k).wait_recv()
            for k in (1, 2, 3):
                w_plane(k).start()

        @pl.when(r == 3)
        def _():
            for k in (1, 2, 3):
                w_plane(k).wait_recv()
            for k in (1, 2, 3):
                w_line(k).wait_send()
            w_core.start()

        @pl.when(r >= 1)
        def _():
            mix_row(r - 1)

        return carry

    loads[5].wait()
    fout_copy.wait_recv()
    lax.fori_loop(0, 5, row_step, 0)

    merged = macc[...].astype(BF)
    mg[0] = merged[0:16]
    mg[1] = merged[16:32]
    gb[z, c] = mg[c]

    def g_copy(k):
        to_z = lax.rem(z + lax.div(k, 2), 8)
        to_c = lax.rem(c + lax.rem(k, 2), 2)
        return remote(
            mg.at[to_c], gb.at[z, c], g_send.at[k], g_recv.at[k], dev(to_z, y, 2 * xh + to_c, core)
        )

    def loop(low, high, action):
        def step(k, carry):
            action(k)
            return carry

        lax.fori_loop(low, high, step, 0)

    loop(1, 16, lambda k: g_copy(k).start())

    prow = iota((256, 256), 0)
    plane_ = iota((256, 256), 1)
    inner = lax.rem(prow, 32)
    column = 24 * lax.div(prow, 32) + inner
    target = jnp.where(plane_ < 128, plane_ + 64, jnp.where(plane_ < 192, plane_ - 128, -1))
    select = ((inner < 24) & (column == target)).astype(F32).astype(BF)
    half = iota((128, 128), 1) < 64

    gain_copy.wait_recv()
    w_core.wait_recv()
    loop(1, 16, lambda k: g_copy(k).wait_recv())
    x0 = gb[:, 0].reshape(128, 512).astype(F32)
    x1 = gb[:, 1].reshape(128, 512).astype(F32)
    square = jnp.sum(x0 * x0, axis=-1, keepdims=True) + jnp.sum(x1 * x1, axis=-1, keepdims=True)
    factor = lax.rsqrt(square * (1.0 / 1024.0) + EPSILON)
    s0 = (x0 * gain_v[0, 0:1, :]).astype(BF)
    s1 = (x1 * gain_v[1, 0:1, :]).astype(BF)
    for g in range(2):
        weights = [
            jnp.concatenate(
                [wb[j % 2, 2 * g + j // 4, 2 * ((j // 2) % 2) + cc] for j in range(8)], axis=0
            )
            for cc in range(2)
        ]
        qkv = (dot_t(s0, weights[0]) + dot_t(s1, weights[1])) * factor
        qkv = dot(qkv.astype(BF), select)
        kv = qkv[:, :128]
        mean = jnp.sum(jnp.where(half, kv * kv, 0.0), axis=-1, keepdims=True) * (1.0 / 64.0)
        kvs[g] = jnp.where(half, kv * (lax.rsqrt(mean + EPSILON) * 0.125), kv).astype(BF)
        query = qkv[:, 128:]
        mean = jnp.sum(query * query, axis=-1, keepdims=True) * (1.0 / 64.0)
        scale = coarse_scales[2 * z + g] * (LOG2E / 8.0)
        qsend[g] = (query * (lax.rsqrt(mean + EPSILON) * scale)).astype(BF)

    def q_copy(k):
        to_xh = lax.rem(xh + lax.div(k, 2), 2)
        to_c = lax.rem(c + lax.rem(k, 2), 2)
        return remote(
            qsend.at[to_c],
            qb.at[xh, c],
            q_send.at[k],
            q_recv.at[k],
            dev(z, y, 2 * to_xh + to_c, core),
        )

    def kv_copy(k):
        to_y = lax.rem(y + lax.div(k, 2), 4)
        to_c = lax.rem(c + lax.rem(k, 2), 2)
        return remote(
            kvs.at[to_c],
            kvb.at[core, y, c],
            kv_send.at[k],
            kv_recv.at[k],
            dev(z, to_y, 2 * xh + to_c, core),
        )

    def forward(k):
        from_y = lax.rem(y + 4 - k, 4)
        return remote(
            kvb.at[core, from_y], kvb.at[core, from_y], fw_send.at[k], fw_recv.at[k], sibling
        )

    loop(1, 4, lambda k: q_copy(k).start())
    loop(1, 8, lambda k: kv_copy(k).start())
    kvb[core, y, c] = kvs[c]
    qb[xh, c] = qsend[c]
    num[...] = jnp.zeros_like(num)
    den[...] = jnp.zeros_like(den)
    loop(1, 4, lambda k: q_copy(k).wait_recv())

    def attend(which, from_y):
        block = kvb[which, from_y].reshape(256, 128)
        weight = jnp.exp2(dot_t(qb[...].reshape(512, 128), block))
        den[...] += weight[:, :128] + weight[:, 128:]
        num[...] += dot(weight.astype(BF), block)

    def direct(k):
        @pl.when(k > 0)
        def _():
            kv_copy(2 * k).wait_recv()

        kv_copy(2 * k + 1).wait_recv()
        forward(k).start()
        attend(core, lax.rem(y + 4 - k, 4))

    def forwarded(k):
        forward(k).wait_recv()
        attend(1 - core, lax.rem(y + 4 - k, 4))

    loop(0, 4, direct)
    loop(0, 4, forwarded)

    half2 = iota((512, 128), 1) < 64
    result = jnp.where(half2, jnp.sum(den[...], axis=-1, keepdims=True), num[...]).astype(BF)
    for hi in range(2):
        for cc in range(2):
            for zz in range(8):
                start = ((hi * 2 + cc) * 8 + zz) * 16
                ob[hi, zz, 16 * cc : 16 * cc + 16] = result[start : start + 16]

    owner_c = lax.div(z, 4)

    def r_copy(k):
        to_z = lax.rem(z + lax.div(k, 2), 8)
        to_xh = lax.rem(xh + lax.rem(k, 2), 2)
        slot = 2 * lax.rem(z, 4) + c
        return remote(
            ob.at[to_xh, to_z],
            rb.at[slot, xh],
            r_send.at[k],
            r_recv.at[2 * slot + xh],
            dev(to_z, y, 2 * to_xh + owner_c, core),
        )

    mine = owner_c == c

    @pl.when(jnp.logical_not(mine))
    def _():
        r_copy(0).start()

    loop(1, 16, lambda k: r_copy(k).start())

    @pl.when(mine)
    def _():
        rb[2 * lax.rem(z, 4) + c, xh] = ob[xh, z]

    own_slot = jnp.where(mine, 2 * (2 * lax.rem(z, 4) + c) + xh, -1)

    def r_wait(s):
        @pl.when(s != own_slot)
        def _():
            remote(
                ob.at[0, 0],
                rb.at[lax.div(s, 2), lax.rem(s, 2)],
                r_send.at[0],
                r_recv.at[s],
                partner,
            ).wait_recv()

    loop(0, 16, r_wait)
    half3 = iota((32, 128), 1) < 64
    for p in range(4):
        even = rb[2 * p, 0].astype(F32) + rb[2 * p, 1].astype(F32)
        odd = rb[2 * p + 1, 0].astype(F32) + rb[2 * p + 1, 1].astype(F32)
        upper = jnp.where(half3, pltpu.roll(even, 64, 1), odd)
        lower = jnp.where(half3, even, pltpu.roll(odd, 64, 1))
        cv_v[:, 128 * p : 128 * p + 128] = (upper / lower).astype(BF)
    cv_copy = pltpu.make_async_copy(cv_v, coarse_out.at[0], load_sem.at[0])
    cv_copy.start()

    for copy in slow_copies + fast_copies + [fout_copy, gain_copy, w_core]:
        copy.wait_send()
    for k in (1, 2, 3):
        w_plane(k).wait_send()

    def finish_row(r):
        att_copy(r).wait_send()
        fine_copy(r).wait()

    loop(0, 4, finish_row)
    loop(1, 16, lambda k: g_copy(k).wait_send())
    loop(1, 4, lambda k: q_copy(k).wait_send())
    loop(1, 8, lambda k: kv_copy(k).wait_send())
    loop(0, 4, lambda k: forward(k).wait_send())

    @pl.when(jnp.logical_not(mine))
    def _():
        r_copy(0).wait_send()

    loop(1, 16, lambda k: r_copy(k).wait_send())
    cv_copy.wait()


def shards(
    image,
    timestep,
    class_label,
    class_table,
    fine_modulation,
    coarse_modulation,
    fine_project,
    fine_output,
    fine_scales,
    merge_weight,
    coarse_project,
    coarse_scales,
):
    smem = pl.BlockSpec(memory_space=pltpu.SMEM)
    hbm = pl.BlockSpec(memory_space=pl.ANY)
    vmem = pltpu.VMEM
    dma = pltpu.SemaphoreType.DMA
    return pl.pallas_call(
        kernel,
        out_shape=(
            jax.ShapeDtypeStruct((4, 128, 256), BF),
            jax.ShapeDtypeStruct((1, 32, 512), BF),
        ),
        in_specs=[smem] * 4 + [hbm] * 8,
        out_specs=(hbm, hbm),
        scratch_shapes=[
            vmem((10, 128, 512), BF),
            vmem((1000, 256), BF),
            vmem((256, 512), BF),
            vmem((256, 512), BF),
            vmem((512, 768), BF),
            vmem((512, 768), BF),
            vmem((2, 256, 512), BF),
            vmem((4, 2048, 512), BF),
            vmem((512, 24), BF),
            vmem((4, 512, 256), BF),
            vmem((10, 128, 256), BF),
            vmem((10, 128, 256), BF),
            vmem((4, 128, 256), BF),
            vmem((4, 128, 256), BF),
            vmem((4, 128, 256), BF),
            vmem((32, 512), F32),
            vmem((2, 16, 512), BF),
            vmem((8, 2, 16, 512), BF),
            vmem((2, 8, 512), F32),
            vmem((2, 4, 4, 32, 512), BF),
            vmem((2, 128, 128), BF),
            vmem((2, 128, 128), BF),
            vmem((2, 4, 2, 128, 128), BF),
            vmem((2, 2, 128, 128), BF),
            vmem((512, 128), F32),
            vmem((512, 128), F32),
            vmem((2, 8, 32, 128), BF),
            vmem((8, 2, 32, 128), BF),
            vmem((32, 512), BF),
            dma((10,)),
            dma((4,)),
            dma((6,)),
            dma((6,)),
            dma((2,)),
            dma((2,)),
            dma((4,)),
            dma((4,)),
            dma((4,)),
            dma((7,)),
            dma((7,)),
            dma((16,)),
            dma((16,)),
            dma((8,)),
            dma((8,)),
            dma((4,)),
            dma((4,)),
            dma((4,)),
            dma((4,)),
            dma((16,)),
            dma((16,)),
        ],
        compiler_params=pltpu.CompilerParams(
            collective_id=0, has_side_effects=True, vmem_limit_bytes=48 * 1024 * 1024
        ),
    )(
        timestep,
        class_label,
        fine_scales,
        coarse_scales,
        image,
        class_table,
        fine_modulation,
        coarse_modulation,
        fine_project,
        fine_output,
        merge_weight.reshape(4, 2048, 512),
        coarse_project,
    )


def solution(mesh):
    in_specs = (
        P("band", None, None),
        P(),
        P(),
        P(),
        P(),
        P(None, "col"),
        P(None, "col"),
        P("col", None),
        P(),
        P(None, "col"),
        P("col", "band"),
        P(),
    )
    out_specs = (P("band", None, "col"), P("band", None, "col"))
    return jax.shard_map(shards, mesh=mesh, in_specs=in_specs, out_specs=out_specs, check_vma=False)
```

time: 306 us -> 71.5 us (0.23)
  waiting for transfers between devices: 192 us -> 0 us
  Pallas kernels: 0 us -> 59.6 us
  starting transfers between devices: 35.3 us -> 0 us
  other arithmetic: 31.5 us -> 0 us
  matrix products: 16.7 us -> 0 us
  between operations: 17.8 us -> 1.95 us
  blocking collectives: 3.77 us -> 0 us
    all_gather x1 -> x0, waiting for transfers between devices: 66.8 us -> none  [shards(): lax.all_gather(coarse_project, 'band', axis=1, tiled=True)]
    pallas_call x0 -> x1, Pallas kernels: none -> 59.6 us  [shards(): pl.pallas_call(kernel, out_shape=(jax.ShapeDtypeStruct((4, 128, 256), BF)...]
    psum x1 -> x0, waiting for transfers between devices: 54.3 us -> none  [shards(): lax.psum(jnp.dot(attended, fine_output, preferred_element_type=jnp.float3...]
    all_to_all x3 -> x0, waiting for transfers between devices: 52.3 us -> none  [the longest x1 29.8 us: shards(): lax.all_to_all(keyval_send, 'band', split_axis=0, concat_axis=0, tiled=True)]
    all_to_all x3 -> x0, starting transfers between devices: 27.2 us -> none  [the longest x1 13.6 us: shards(): lax.all_to_all(query_send, 'band', split_axis=0, concat_axis=0, tiled=True)]
    reduce_sum x10 -> x0, other arithmetic: 17.4 us -> none  [the longest x5 14.4 us: shards(): logits = scales_local * jnp.sum(queries * key_win, axis=-1)]
    dot_general x9 -> x0, matrix products: 16.7 us -> none  [the longest x1 5.02 us: shards(): jnp.dot(patches, merge_weight, preferred_element_type=jnp.float32)]
    convert_element_type x8 -> x0, other arithmetic: 9.76 us -> none  [the longest x1 4.65 us: shards(): (numerator / denominator[:, :, :, None]).astype(jnp.bfloat16)]
  transfers between devices with their start and end apart: 8 -> 0, of which waited for: 8 -> 0; matrix products, arithmetic and copies ran while one was open for 4% -> 0% of each run, Pallas kernels for 0% -> 0%
where the time goes in v1:
time: 71.5 us; the launch traced here: 71.1 us
  Pallas kernels  59.6 us (83%)
  local copies, waits for them, and re-layouts  9.54 us (13%)
  between operations  1.95 us (3%)
    pallas_call x1, Pallas kernels, shards(): pl.pallas_call(kernel, out_shape=(jax.ShapeDtypeStruct((4, 128, 256), BF)...  59.6 us
    unnamed x19, local copies, waits for them, and re-layouts  9.54 us

profile of v1, /device:TPU:1, one launch (start us, length us, event | category | flops | bytes accessed | tf_op | source)
XLA Modules:
  0.0 71.1 jit_solution(4684644886319562437)
XLA Ops:
  1.9 0.9 %copy.14.coarse_project = bf16[512,24]{1,0:T(8,128)(2,1)S(1)} copy(bf16[512,24]{0,1:T(8,128)(2,1)} %param.22) | data formatting | bytes 49152 | tf_op args[10]
  2.8 0.0 copy-start
  2.8 1.1 %copy-done = bf16[512,768]{1,0:T(8,128)(2,1)S(1)} copy-done((bf16[512,768]{1,0:T(8,128)(2,1)S(1)}, bf16[512,768]{1,0:T(8,128)(2,1)}, u32[]{:S(2)}) %copy-start) | copy-done | bytes 786456
  3.9 0.0 copy-start.1
  3.9 1.0 %copy-done.1 = bf16[4,128,512]{2,1,0:T(8,128)(2,1)S(1)} copy-done((bf16[4,128,512]{2,1,0:T(8,128)(2,1)S(1)}, bf16[4,128,512]{2,1,0:T(8,128)(2,1)}, u32[]{:S(2)}) %copy-start.1) | copy-done | bytes 524312
  5.0 0.0 copy-start.2
  5.0 1.0 %copy-done.2 = bf16[1000,256]{1,0:T(8,128)(2,1)S(1)} copy-done((bf16[1000,256]{1,0:T(8,128)(2,1)S(1)}, bf16[1000,256]{1,0:T(8,128)(2,1)}, u32[]{:S(2)}) %copy-start.2) | copy-done | bytes 512024
  6.0 0.0 copy-start.3
  6.0 0.9 %copy-done.3 = bf16[256,512]{1,0:T(8,128)(2,1)S(1)} copy-done((bf16[256,512]{1,0:T(8,128)(2,1)S(1)}, bf16[256,512]{1,0:T(8,128)(2,1)}, u32[]{:S(2)}) %copy-start.3) | copy-done | bytes 262168
  7.0 0.0 copy-start.4
  7.0 0.9 %copy-done.4 = bf16[256,512]{1,0:T(8,128)(2,1)S(1)} copy-done((bf16[256,512]{1,0:T(8,128)(2,1)S(1)}, bf16[256,512]{1,0:T(8,128)(2,1)}, u32[]{:S(2)}) %copy-start.4) | copy-done | bytes 262168
  7.9 0.0 copy-start.5
  7.9 0.9 %copy-done.5 = bf16[256,512]{1,0:T(8,128)(2,1)S(1)} copy-done((bf16[256,512]{1,0:T(8,128)(2,1)S(1)}, bf16[256,512]{1,0:T(8,128)(2,1)}, u32[]{:S(2)}) %copy-start.5) | copy-done | bytes 262168
  8.9 0.0 copy-start.6
  8.9 0.7 copy-done.6
  9.5 0.0 copy-start.7
  9.5 0.7 copy-done.7
  10.2 59.6 %shard_map.131 = (bf16[4,128,256]{2,1,0:T(8,128)(2,1)S(1)}, bf16[1,32,512]{2,1,0:T(8,128)(2,1)S(1)}) custom-call(s32[1]{0:T(128)S(6)} %copy.17.timestep, s32[1]{0:T(128)S(6)} %copy.18.label, f32[8]{0:T(128)S(1)} %copy-done.6, f32[16]{0:T(128)S(1)} %copy-done.7, bf16[4,128,512]{2,1,0:T(8,128)(2,1)S(1)} %copy-done.1, bf16[1000,256]{1,0:T(8,128)(2,1)S(1)} %copy-done.2, ...), custom_call_target="tpu_custom_call" | custom-call | tf_op jit(solution)/shard_map/pallas_call | solution.py:586
  69.8 0.7 copy.19
  70.5 0.6 copy.20
Async XLA Ops:
  2.8 1.1 %copy-start = (bf16[512,768]{1,0:T(8,128)(2,1)S(1)}, bf16[512,768]{1,0:T(8,128)(2,1)}, u32[]{:S(2)}) copy-start(bf16[512,768]{1,0:T(8,128)(2,1)} %fine_project.1) | copy-start | bytes 2359300
  3.9 1.0 %copy-start.1 = (bf16[4,128,512]{2,1,0:T(8,128)(2,1)S(1)}, bf16[4,128,512]{2,1,0:T(8,128)(2,1)}, u32[]{:S(2)}) copy-start(bf16[4,128,512]{2,1,0:T(8,128)(2,1)} %image.1) | copy-start | bytes 1572868
  5.0 1.0 %copy-start.2 = (bf16[1000,256]{1,0:T(8,128)(2,1)S(1)}, bf16[1000,256]{1,0:T(8,128)(2,1)}, u32[]{:S(2)}) copy-start(bf16[1000,256]{1,0:T(8,128)(2,1)} %class_table.1) | copy-start | bytes 1536004
  6.0 0.9 %copy-start.3 = (bf16[256,512]{1,0:T(8,128)(2,1)S(1)}, bf16[256,512]{1,0:T(8,128)(2,1)}, u32[]{:S(2)}) copy-start(bf16[256,512]{1,0:T(8,128)(2,1)} %fine_modulation.1) | copy-start | bytes 786436
  7.0 0.9 %copy-start.4 = (bf16[256,512]{1,0:T(8,128)(2,1)S(1)}, bf16[256,512]{1,0:T(8,128)(2,1)}, u32[]{:S(2)}) copy-start(bf16[256,512]{1,0:T(8,128)(2,1)} %coarse_modulation.1) | copy-start | bytes 786436
  7.9 0.9 %copy-start.5 = (bf16[256,512]{1,0:T(8,128)(2,1)S(1)}, bf16[256,512]{1,0:T(8,128)(2,1)}, u32[]{:S(2)}) copy-start(bf16[256,512]{1,0:T(8,128)(2,1)} %fine_output.1) | copy-start | bytes 786436
  8.9 0.7 copy-start.6
  9.5 0.7 copy-start.7

commit v2 on v1

--- a/solution.py
+++ b/solution.py
@@ -28,10 +28,10 @@
 
 
 def kernel(
-    timestep,
-    label,
-    fine_scales,
-    coarse_scales,
+    timestep_h,
+    label_h,
+    fine_scales_h,
+    coarse_scales_h,
     image,
     class_table,
     fine_modulation,
@@ -57,10 +57,10 @@
     att_own,
     att_got,
     fine_v,
-    macc,
     mg,
     gb,
     gain_v,
+    wst,
     wb,
     kvs,
     qsend,
@@ -71,6 +71,11 @@
     ob,
     rb,
     cv_v,
+    timestep,
+    label,
+    fine_scales,
+    coarse_scales,
+    entered,
     load_sem,
     merge_sem,
     halo_send,
@@ -122,6 +127,14 @@
         load(coarse_project, cproj_v, 8),
         load(fine_output, fout_v.at[c], 9),
     ]
+    scalars = [
+        load(timestep_h, timestep, 10),
+        load(label_h, label, 11),
+        load(fine_scales_h, fine_scales, 12),
+        load(coarse_scales_h, coarse_scales, 13),
+    ]
+    for copy in scalars:
+        copy.start()
     rows = [load(image.at[row_of(u)], xb.at[3 + u], u) for u in range(4)]
     merges = [
         pltpu.make_async_copy(merge_weight.at[row_of(u)], merge_v.at[u], merge_sem.at[u])
@@ -139,20 +152,34 @@
     def signal(device):
         pl.semaphore_signal(barrier, inc=1, device_id=device, device_id_type=MESH)
 
-    signal(slow)
-    signal(sibling)
-
-    def signal_line(k, carry):
-        signal(dev(lax.rem(z + lax.div(k, 4), 8), y, lax.rem(x + lax.rem(k, 4), 4), core))
-        return carry
-
-    def signal_plane(k, carry):
-        signal(dev(z, lax.rem(y + lax.div(k, 4), 4), lax.rem(x + lax.rem(k, 4), 4), core))
-        return carry
-
-    lax.fori_loop(1, 32, signal_line, 0)
-    lax.fori_loop(4, 16, signal_plane, 0)
-    pl.semaphore_wait(barrier, 45)
+    def near(dz, dy, dx):
+        return dev(lax.rem(z + 8 + dz, 8), lax.rem(y + 4 + dy, 4), lax.rem(x + 4 + dx, 4), core)
+
+    nearest = [near(*d) for d in ((0, 0, 1), (0, 0, -1), (0, 1, 0), (0, -1, 0), (1, 0, 0), (-1, 0, 0))]
+    for device in [slow, sibling] + nearest:
+        signal(device)
+
+    move_z = lax.rem(2 * z + lax.div(y, 2), 8)
+    move_y = 2 * lax.div(z, 4) + lax.rem(y, 2)
+    moves = (move_z != z) | (move_y != y)
+    mover = dev(move_z, move_y, x, core)
+
+    pl.semaphore_wait(barrier, 8)
+
+    def vouch(step, devices):
+        for device in devices:
+            pl.semaphore_signal(
+                entered.at[step], inc=1, device_id=device, device_id_type=MESH
+            )
+
+    pending = []
+
+    def loop(low, high, action):
+        def step(k, carry):
+            action(k)
+            return carry
+
+        lax.fori_loop(low, high, step, 0)
 
     def remote(src, dst, send, recv, device):
         return pltpu.make_async_remote_copy(
@@ -178,14 +205,39 @@
     ]
     for copy in slow_copies + fast_copies:
         copy.start()
-    fout_copy = remote(fine_output, fout_v.at[c], pair_send.at[0], pair_recv.at[0], partner)
+    pending.extend(copy.wait_send for copy in slow_copies + fast_copies)
+    fout_copy = remote(
+        fine_output.at[core], fout_v.at[c, core], pair_send.at[0], pair_recv.at[0], partner
+    )
+    fout_pass = remote(
+        fout_v.at[1 - c, core],
+        fout_v.at[1 - c, core],
+        pair_send.at[2],
+        pair_recv.at[2],
+        sibling,
+    )
     fout_copy.start()
+    pending.append(fout_copy.wait_send)
+    vouch(0, nearest)
     for copy in merges:
         copy.start()
 
     loads[4].wait()
-    eye = (iota((32, 24), 0) == iota((32, 24), 1)).astype(BF)
-    wb[core, y, x] = dot_t(eye, cproj_v[...]).astype(BF)
+    wst[...] = jnp.concatenate(
+        [cproj_v[...].astype(F32), jnp.zeros((8, 512), F32)], axis=0
+    ).astype(BF)
+    w_move = remote(wst, wb.at[core, move_y, x], w_send.at[7], w_recv.at[7], mover)
+
+    @pl.when(jnp.logical_not(moves))
+    def _():
+        wb[core, y, x] = wst[...]
+
+    def w_move_done():
+        @pl.when(moves)
+        def _():
+            w_move.wait_send()
+
+    pending.append(w_move_done)
 
     def w_line(k):
         return remote(
@@ -206,9 +258,8 @@
         )
 
     w_core = remote(wb.at[core], wb.at[core], w_send.at[0], w_recv.at[0], sibling)
-    for k in (1, 2, 3):
-        w_line(k).start()
-
+    for copy in scalars:
+        copy.wait()
     lane = iota((8, 256), 1)
     freq = jnp.exp((-math.log(10000.0) / 128.0) * lax.rem(lane, 128).astype(F32))
     angle = timestep[0].astype(F32) * freq
@@ -230,6 +281,10 @@
     gain_v[c] = gain_of(cmod_v[...])
     gain_copy = remote(gain_v.at[c], gain_v.at[c], pair_send.at[1], pair_recv.at[1], partner)
     gain_copy.start()
+    pending.append(gain_copy.wait_send)
+
+    pl.semaphore_wait(entered.at[0], 6)
+    vouch(1, [near(2, 0, 0), near(-2, 0, 0), near(0, 2, 0)])
 
     loads[2].wait()
     fp = fproj_v[...]
@@ -271,18 +326,23 @@
     query = dot(normed, wperm[:, 0:256]).astype(BF).astype(F32)
     query = query * unit_factor(query) * q_scale
     for h in range(4):
-        qs[:, 128 * h : 128 * h + 128, :] = (
-            jnp.where(lane_head == h, query, 0.0).astype(BF).reshape(4, 128, 256)
-        )
+        masked = jnp.where(lane_head == h, query, 0.0).astype(BF).reshape(4, 4, 32, 256)
+        qs[:, :, 32 * h : 32 * h + 32, :] = masked
+    pl.semaphore_wait(entered.at[1], 3)
+    vouch(2, [near(0, 0, 1), near(0, 0, -1), near(0, 0, 2), near(0, 2, 0)])
     for copy in fast_copies:
         copy.wait_recv()
     key, value = keys_values(normed_of(xb[0:3].reshape(384, 512)))
     kb[0:3] = key.reshape(3, 128, 256)
     vb[0:3] = value.reshape(3, 128, 256)
 
-    distance = iota((128, 128), 0) - iota((128, 128), 1)
-    far = jnp.where((distance <= 3) & (distance >= -3), 0.0, -1e30)
-    macc[...] = jnp.zeros_like(macc)
+    first = (0, 16, 48, 64)
+    column_gap = iota((32, 448), 0) - lax.rem(iota((32, 448), 1), 64)
+    far = []
+    for b in range(4):
+        gap = column_gap + (32 * b - first[b])
+        far.append(jnp.where((gap <= 3) & (gap >= -3), 0.0, -1e30))
+    key_row = lax.div(iota((1, 448), 1), 64) - 3
     perm = (iota((128, 128), 1) == 4 * lax.rem(iota((128, 128), 0), 32) + lax.div(iota((128, 128), 0), 32)).astype(F32).astype(BF)
 
     def att_copy(r):
@@ -292,86 +352,83 @@
         return pltpu.make_async_copy(fine_v.at[r], fine_out.at[row_of(r)], fine_sem.at[r])
 
     def attend_row(r):
-        keys = kb[pl.ds(r, 7)].reshape(896, 256)
-        values = vb[pl.ds(r, 7)].reshape(896, 256)
-        bias = []
-        for d in range(7):
-            row = 4 * band + row_of(r + d - 3)
-            outside = jnp.where((row < 0) | (row >= 4 * BANDS), -1e30, 0.0)
-            bias.append(far + outside)
-        bias = jnp.concatenate(bias, axis=1)
-        logits = dot_t(qs[r], keys).reshape(4, 128, 896) + bias[None]
-        weight = jnp.exp2(logits)
-        total = jnp.sum(weight, axis=-1, keepdims=True)
-        out = dot(weight.astype(BF).reshape(512, 896), values).reshape(4, 128, 256) * (1.0 / total)
-        mixed = jnp.zeros((128, 256), F32)
-        for h in range(4):
-            mixed = jnp.where(lane_head == h, out[h], mixed)
-        att_own[r] = mixed.astype(BF)
+        slot = key_row + r
+        row = 4 * band + slot + (1 - core) * (3 - 2 * slot)
+        outside = jnp.where((row < 0) | (row >= 4 * BANDS), -1e30, 0.0)
+        for b in range(4):
+            keys = kb[pl.ds(r, 7), first[b] : first[b] + 64].reshape(448, 256)
+            values = vb[pl.ds(r, 7), first[b] : first[b] + 64].reshape(448, 256)
+            logits = dot_t(qs[r, b], keys).reshape(4, 32, 448) + (far[b] + outside)[None]
+            weight = jnp.exp2(logits)
+            total = jnp.sum(weight, axis=-1, keepdims=True)
+            out = dot(weight.astype(BF).reshape(128, 448), values).reshape(4, 32, 256)
+            out = out * (1.0 / total)
+            mixed = jnp.zeros((32, 256), F32)
+            for h in range(4):
+                mixed = jnp.where(lane_head == h, out[h], mixed)
+            att_own[r, 32 * b : 32 * b + 32] = mixed.astype(BF)
         att_copy(r).start()
 
     def mix_row(r):
-        att_copy(r).wait_recv()
-        merge_copy = pltpu.make_async_copy(
-            merge_weight.at[row_of(r)], merge_v.at[r], merge_sem.at[r]
-        )
-        merge_copy.wait()
-        full = (
-            xb[3 + r].astype(F32) + dot(att_own[r], fout_v[c]) + dot(att_got[r], fout_v[1 - c])
-        )
+        full = xb[3 + r].astype(F32) + dot(att_own[r], fout_v[c].reshape(256, 512))
+        full = full + dot(att_got[r], fout_v[1 - c].reshape(256, 512))
         fine_v[r] = jnp.where(c == 0, full[:, :256], full[:, 256:]).astype(BF)
-        fine_copy(r).start()
         patches = dot(perm, full.astype(BF)).astype(BF)
-        part = macc[...]
+        part = jnp.zeros((32, 512), F32)
         for p in range(4):
             part = part + dot(patches[32 * p : 32 * p + 32], merge_v[r, 512 * p : 512 * p + 512, :])
-        macc[...] = part
-
-    def row_step(r, carry):
-        @pl.when((r >= 1) & (r < 4))
-        def _():
-            slow_copy = remote(
-                image.at[row_of(4 - r)],
-                xb.at[6 + r],
-                halo_send.at[r - 1],
-                halo_recv.at[r - 1],
-                slow,
-            )
-            slow_copy.wait_recv()
-            key, value = keys_values(normed_of(xb[6 + r]))
-            kb[6 + r] = key
-            vb[6 + r] = value
-
-        @pl.when(r < 4)
-        def _():
-            attend_row(r)
-
-        @pl.when(r == 1)
-        def _():
-            for k in (1, 2, 3):
-                w_line(k).wait_recv()
-            for k in (1, 2, 3):
-                w_plane(k).start()
-
-        @pl.when(r == 3)
-        def _():
-            for k in (1, 2, 3):
-                w_plane(k).wait_recv()
-            for k in (1, 2, 3):
-                w_line(k).wait_send()
-            w_core.start()
-
-        @pl.when(r >= 1)
-        def _():
-            mix_row(r - 1)
-
-        return carry
+        return part
+
+    def new_row(r):
+        slow_copies[r - 1].wait_recv()
+        key, value = keys_values(normed_of(xb[6 + r]))
+        kb[6 + r] = key
+        vb[6 + r] = value
+
+    attend_row(0)
+    pl.semaphore_wait(entered.at[2], 4)
+
+    @pl.when(moves)
+    def _():
+        w_move.start()
 
     loads[5].wait()
     fout_copy.wait_recv()
-    lax.fori_loop(0, 5, row_step, 0)
-
-    merged = macc[...].astype(BF)
+    fout_pass.start()
+    pending.append(fout_pass.wait_send)
+    new_row(1)
+    attend_row(1)
+
+    @pl.when(moves)
+    def _():
+        w_move.wait_recv()
+
+    for k in (2, 1, 3):
+        w_line(k).start()
+    new_row(2)
+    attend_row(2)
+    for k in (1, 2, 3):
+        w_line(k).wait_recv()
+    for k in (2, 1, 3):
+        w_plane(k).start()
+    new_row(3)
+    attend_row(3)
+    fout_pass.wait_recv()
+    for copy in merges:
+        copy.wait()
+    for r in range(3):
+        att_copy(r).wait_recv()
+    merged = mix_row(0) + mix_row(1) + mix_row(2)
+    att_copy(3).wait_recv()
+    merged = (merged + mix_row(3)).astype(BF)
+    pending.extend(w_plane(k).wait_send for k in (1, 2, 3))
+
+    def finish_row(r):
+        att_copy(r).wait_send()
+        fine_copy(r).wait()
+
+    pending.append(lambda: loop(0, 4, finish_row))
+
     mg[0] = merged[0:16]
     mg[1] = merged[16:32]
     gb[z, c] = mg[c]
@@ -383,14 +440,16 @@
             mg.at[to_c], gb.at[z, c], g_send.at[k], g_recv.at[k], dev(to_z, y, 2 * xh + to_c, core)
         )
 
-    def loop(low, high, action):
-        def step(k, carry):
-            action(k)
-            return carry
-
-        lax.fori_loop(low, high, step, 0)
-
     loop(1, 16, lambda k: g_copy(k).start())
+    for k in (1, 2, 3):
+        w_plane(k).wait_recv()
+    for k in (1, 2, 3):
+        w_line(k).wait_send()
+    w_core.start()
+    pending.append(w_core.wait_send)
+    pending.append(lambda: loop(1, 16, lambda k: g_copy(k).wait_send()))
+    for r in range(4):
+        fine_copy(r).start()
 
     prow = iota((256, 256), 0)
     plane_ = iota((256, 256), 1)
@@ -423,7 +482,7 @@
         kvs[g] = jnp.where(half, kv * (lax.rsqrt(mean + EPSILON) * 0.125), kv).astype(BF)
         query = qkv[:, 128:]
         mean = jnp.sum(query * query, axis=-1, keepdims=True) * (1.0 / 64.0)
-        scale = coarse_scales[2 * z + g] * (LOG2E / 8.0)
+        scale = coarse_scales[z + 8 * g] * (LOG2E / 8.0)
         qsend[g] = (query * (lax.rsqrt(mean + EPSILON) * scale)).astype(BF)
 
     def q_copy(k):
@@ -454,8 +513,11 @@
             kvb.at[core, from_y], kvb.at[core, from_y], fw_send.at[k], fw_recv.at[k], sibling
         )
 
+    for k in (4, 5, 2, 3, 6, 7, 1):
+        kv_copy(k).start()
     loop(1, 4, lambda k: q_copy(k).start())
-    loop(1, 8, lambda k: kv_copy(k).start())
+    pending.append(lambda: loop(1, 4, lambda k: q_copy(k).wait_send()))
+    pending.append(lambda: loop(1, 8, lambda k: kv_copy(k).wait_send()))
     kvb[core, y, c] = kvs[c]
     qb[xh, c] = qsend[c]
     num[...] = jnp.zeros_like(num)
@@ -483,6 +545,7 @@
 
     loop(0, 4, direct)
     loop(0, 4, forwarded)
+    pending.append(lambda: loop(0, 4, lambda k: forward(k).wait_send()))
 
     half2 = iota((512, 128), 1) < 64
     result = jnp.where(half2, jnp.sum(den[...], axis=-1, keepdims=True), num[...]).astype(BF)
@@ -492,46 +555,32 @@
                 start = ((hi * 2 + cc) * 8 + zz) * 16
                 ob[hi, zz, 16 * cc : 16 * cc + 16] = result[start : start + 16]
 
-    owner_c = lax.div(z, 4)
-
     def r_copy(k):
         to_z = lax.rem(z + lax.div(k, 2), 8)
         to_xh = lax.rem(xh + lax.rem(k, 2), 2)
-        slot = 2 * lax.rem(z, 4) + c
         return remote(
             ob.at[to_xh, to_z],
-            rb.at[slot, xh],
+            rb.at[z, xh],
             r_send.at[k],
-            r_recv.at[2 * slot + xh],
-            dev(to_z, y, 2 * to_xh + owner_c, core),
-        )
-
-    mine = owner_c == c
-
-    @pl.when(jnp.logical_not(mine))
-    def _():
-        r_copy(0).start()
+            r_recv.at[k],
+            dev(to_z, y, 2 * to_xh + c, core),
+        )
+
+    def r_from(k):
+        from_z = lax.rem(z + 8 - lax.div(k, 2), 8)
+        from_xh = lax.rem(xh + lax.rem(k, 2), 2)
+        return remote(
+            ob.at[from_xh, from_z],
+            rb.at[from_z, from_xh],
+            r_send.at[k],
+            r_recv.at[k],
+            dev(from_z, y, 2 * from_xh + c, core),
+        )
 
     loop(1, 16, lambda k: r_copy(k).start())
-
-    @pl.when(mine)
-    def _():
-        rb[2 * lax.rem(z, 4) + c, xh] = ob[xh, z]
-
-    own_slot = jnp.where(mine, 2 * (2 * lax.rem(z, 4) + c) + xh, -1)
-
-    def r_wait(s):
-        @pl.when(s != own_slot)
-        def _():
-            remote(
-                ob.at[0, 0],
-                rb.at[lax.div(s, 2), lax.rem(s, 2)],
-                r_send.at[0],
-                r_recv.at[s],
-                partner,
-            ).wait_recv()
-
-    loop(0, 16, r_wait)
+    pending.append(lambda: loop(1, 16, lambda k: r_copy(k).wait_send()))
+    rb[z, xh] = ob[xh, z]
+    loop(1, 16, lambda k: r_from(k).wait_recv())
     half3 = iota((32, 128), 1) < 64
     for p in range(4):
         even = rb[2 * p, 0].astype(F32) + rb[2 * p, 1].astype(F32)
@@ -542,27 +591,9 @@
     cv_copy = pltpu.make_async_copy(cv_v, coarse_out.at[0], load_sem.at[0])
     cv_copy.start()
 
-    for copy in slow_copies + fast_copies + [fout_copy, gain_copy, w_core]:
-        copy.wait_send()
-    for k in (1, 2, 3):
-        w_plane(k).wait_send()
-
-    def finish_row(r):
-        att_copy(r).wait_send()
-        fine_copy(r).wait()
-
-    loop(0, 4, finish_row)
-    loop(1, 16, lambda k: g_copy(k).wait_send())
-    loop(1, 4, lambda k: q_copy(k).wait_send())
-    loop(1, 8, lambda k: kv_copy(k).wait_send())
-    loop(0, 4, lambda k: forward(k).wait_send())
-
-    @pl.when(jnp.logical_not(mine))
-    def _():
-        r_copy(0).wait_send()
-
-    loop(1, 16, lambda k: r_copy(k).wait_send())
-    cv_copy.wait()
+    pending.append(cv_copy.wait)
+    for wait in pending:
+        wait()
 
 
 def shards(
@@ -579,9 +610,9 @@
     coarse_project,
     coarse_scales,
 ):
-    smem = pl.BlockSpec(memory_space=pltpu.SMEM)
     hbm = pl.BlockSpec(memory_space=pl.ANY)
     vmem = pltpu.VMEM
+    smem = pltpu.SMEM
     dma = pltpu.SemaphoreType.DMA
     return pl.pallas_call(
         kernel,
@@ -589,7 +620,7 @@
             jax.ShapeDtypeStruct((4, 128, 256), BF),
             jax.ShapeDtypeStruct((1, 32, 512), BF),
         ),
-        in_specs=[smem] * 4 + [hbm] * 8,
+        in_specs=[hbm] * 12,
         out_specs=(hbm, hbm),
         scratch_shapes=[
             vmem((10, 128, 512), BF),
@@ -598,19 +629,19 @@
             vmem((256, 512), BF),
             vmem((512, 768), BF),
             vmem((512, 768), BF),
-            vmem((2, 256, 512), BF),
+            vmem((2, 2, 128, 512), BF),
             vmem((4, 2048, 512), BF),
-            vmem((512, 24), BF),
-            vmem((4, 512, 256), BF),
+            vmem((24, 512), BF),
+            vmem((4, 4, 128, 256), BF),
             vmem((10, 128, 256), BF),
             vmem((10, 128, 256), BF),
             vmem((4, 128, 256), BF),
             vmem((4, 128, 256), BF),
             vmem((4, 128, 256), BF),
-            vmem((32, 512), F32),
             vmem((2, 16, 512), BF),
             vmem((8, 2, 16, 512), BF),
             vmem((2, 8, 512), F32),
+            vmem((32, 512), BF),
             vmem((2, 4, 4, 32, 512), BF),
             vmem((2, 128, 128), BF),
             vmem((2, 128, 128), BF),
@@ -621,17 +652,22 @@
             vmem((2, 8, 32, 128), BF),
             vmem((8, 2, 32, 128), BF),
             vmem((32, 512), BF),
-            dma((10,)),
+            smem((1,), jnp.int32),
+            smem((1,), jnp.int32),
+            smem((8,), F32),
+            smem((16,), F32),
+            pltpu.SemaphoreType.REGULAR((3,)),
+            dma((14,)),
             dma((4,)),
             dma((6,)),
             dma((6,)),
-            dma((2,)),
-            dma((2,)),
+            dma((3,)),
+            dma((3,)),
             dma((4,)),
             dma((4,)),
             dma((4,)),
-            dma((7,)),
-            dma((7,)),
+            dma((8,)),
+            dma((8,)),
             dma((16,)),
             dma((16,)),
             dma((8,)),
@@ -644,7 +680,7 @@
             dma((16,)),
         ],
         compiler_params=pltpu.CompilerParams(
-            collective_id=0, has_side_effects=True, vmem_limit_bytes=48 * 1024 * 1024
+            collective_id=0, has_side_effects=True, vmem_limit_bytes=62 * 1024 * 1024
         ),
     )(
         timestep,
@@ -656,9 +692,9 @@
         fine_modulation,
         coarse_modulation,
         fine_project,
-        fine_output,
+        fine_output.reshape(2, 128, 512),
         merge_weight.reshape(4, 2048, 512),
-        coarse_project,
+        coarse_project.T,
     )
 
 

time: 71.5 us -> 60.4 us (0.84)
  local copies, waits for them, and re-layouts: 9.54 us -> 3.04 us
  Pallas kernels: 59.6 us -> 54.6 us
    unnamed x19 -> x2, local copies, waits for them, and re-layouts: 9.54 us -> 3.04 us
    pallas_call x1, Pallas kernels: 59.6 us -> 54.6 us  [shards(): pl.pallas_call(kernel, out_shape=(jax.ShapeDtypeStruct((4, 128, 256), BF)...]
where the time goes in v2:
time: 60.4 us; the launch traced here: 59.6 us
  Pallas kernels  54.6 us (90%)
  local copies, waits for them, and re-layouts  3.04 us (5%)
  between operations  1.93 us (3%)
    pallas_call x1, Pallas kernels, shards(): pl.pallas_call(kernel, out_shape=(jax.ShapeDtypeStruct((4, 128, 256), BF)...  54.6 us
    unnamed x2, local copies, waits for them, and re-layouts  3.04 us

profile of v2, /device:TPU:1, one launch (start us, length us, event | category | flops | bytes accessed | tf_op | source)
XLA Modules:
  0.0 59.6 jit_solution(1051270438144047258)
XLA Ops:
  1.9 54.6 %shard_map.131 = (bf16[4,128,256]{2,1,0:T(8,128)(2,1)}, bf16[1,32,512]{2,1,0:T(8,128)(2,1)}) custom-call(s32[1]{0:T(128)S(6)} %copy.16.timestep_h, s32[1]{0:T(128)S(6)} %copy.17.label_h, f32[8]{0:T(128)} %fine_scales_h.1, f32[16]{0:T(128)} %coarse_scales_h.1, bf16[4,128,512]{2,1,0:T(8,128)(2,1)} %image.1, bf16[1000,256]{1,0:T(8,128)(2,1)} %class_table.1, ...), custom_call_target="tpu_custom_call" | custom-call | tf_op jit(solution)/shard_map/pallas_call | solution.py:617
  56.5 1.7 %copy.18 = bf16[4,128,256]{2,1,0:T(8,128)(2,1)} copy(bf16[4,128,256]{2,1,0:T(8,128)(2,1)} %get-tuple-element.4) | data formatting | bytes 524288
  58.2 1.4 %copy.19 = bf16[1,32,512]{2,1,0:T(8,128)(2,1)} copy(bf16[1,32,512]{2,1,0:T(8,128)(2,1)} %get-tuple-element.5) | data formatting | bytes 65536

commit v3 on v2

--- a/solution.py
+++ b/solution.py
@@ -56,11 +56,9 @@
     vb,
     att_own,
     att_got,
-    fine_v,
     mg,
     gb,
     gain_v,
-    wst,
     wb,
     kvs,
     qsend,
@@ -70,7 +68,6 @@
     den,
     ob,
     rb,
-    cv_v,
     timestep,
     label,
     fine_scales,
@@ -159,11 +156,6 @@
     for device in [slow, sibling] + nearest:
         signal(device)
 
-    move_z = lax.rem(2 * z + lax.div(y, 2), 8)
-    move_y = 2 * lax.div(z, 4) + lax.rem(y, 2)
-    moves = (move_z != z) | (move_y != y)
-    mover = dev(move_z, move_y, x, core)
-
     pl.semaphore_wait(barrier, 8)
 
     def vouch(step, devices):
@@ -223,21 +215,9 @@
         copy.start()
 
     loads[4].wait()
-    wst[...] = jnp.concatenate(
+    wb[core, y, x] = jnp.concatenate(
         [cproj_v[...].astype(F32), jnp.zeros((8, 512), F32)], axis=0
     ).astype(BF)
-    w_move = remote(wst, wb.at[core, move_y, x], w_send.at[7], w_recv.at[7], mover)
-
-    @pl.when(jnp.logical_not(moves))
-    def _():
-        wb[core, y, x] = wst[...]
-
-    def w_move_done():
-        @pl.when(moves)
-        def _():
-            w_move.wait_send()
-
-    pending.append(w_move_done)
 
     def w_line(k):
         return remote(
@@ -283,9 +263,6 @@
     gain_copy.start()
     pending.append(gain_copy.wait_send)
 
-    pl.semaphore_wait(entered.at[0], 6)
-    vouch(1, [near(2, 0, 0), near(-2, 0, 0), near(0, 2, 0)])
-
     loads[2].wait()
     fp = fproj_v[...]
     for part in range(3):
@@ -328,8 +305,6 @@
     for h in range(4):
         masked = jnp.where(lane_head == h, query, 0.0).astype(BF).reshape(4, 4, 32, 256)
         qs[:, :, 32 * h : 32 * h + 32, :] = masked
-    pl.semaphore_wait(entered.at[1], 3)
-    vouch(2, [near(0, 0, 1), near(0, 0, -1), near(0, 0, 2), near(0, 2, 0)])
     for copy in fast_copies:
         copy.wait_recv()
     key, value = keys_values(normed_of(xb[0:3].reshape(384, 512)))
@@ -347,9 +322,6 @@
 
     def att_copy(r):
         return remote(att_own.at[r], att_got.at[r], att_send.at[r], att_recv.at[r], partner)
-
-    def fine_copy(r):
-        return pltpu.make_async_copy(fine_v.at[r], fine_out.at[row_of(r)], fine_sem.at[r])
 
     def attend_row(r):
         slot = key_row + r
@@ -372,7 +344,7 @@
     def mix_row(r):
         full = xb[3 + r].astype(F32) + dot(att_own[r], fout_v[c].reshape(256, 512))
         full = full + dot(att_got[r], fout_v[1 - c].reshape(256, 512))
-        fine_v[r] = jnp.where(c == 0, full[:, :256], full[:, 256:]).astype(BF)
+        fine_out[row_of(r)] = jnp.where(c == 0, full[:, :256], full[:, 256:]).astype(BF)
         patches = dot(perm, full.astype(BF)).astype(BF)
         part = jnp.zeros((32, 512), F32)
         for p in range(4):
@@ -386,33 +358,26 @@
         vb[6 + r] = value
 
     attend_row(0)
-    pl.semaphore_wait(entered.at[2], 4)
-
-    @pl.when(moves)
-    def _():
-        w_move.start()
-
+    pl.semaphore_wait(entered.at[0], 6)
+    vouch(1, [near(2, 0, 0), near(-2, 0, 0), near(0, 2, 0)])
     loads[5].wait()
     fout_copy.wait_recv()
     fout_pass.start()
     pending.append(fout_pass.wait_send)
     new_row(1)
     attend_row(1)
-
-    @pl.when(moves)
-    def _():
-        w_move.wait_recv()
-
+    pl.semaphore_wait(entered.at[1], 3)
+    vouch(2, [near(0, 0, 1), near(0, 0, -1), near(0, 0, 2)])
     for k in (2, 1, 3):
         w_line(k).start()
     new_row(2)
     attend_row(2)
+    new_row(3)
+    attend_row(3)
     for k in (1, 2, 3):
         w_line(k).wait_recv()
     for k in (2, 1, 3):
         w_plane(k).start()
-    new_row(3)
-    attend_row(3)
     fout_pass.wait_recv()
     for copy in merges:
         copy.wait()
@@ -421,11 +386,11 @@
     merged = mix_row(0) + mix_row(1) + mix_row(2)
     att_copy(3).wait_recv()
     merged = (merged + mix_row(3)).astype(BF)
+    pl.semaphore_wait(entered.at[2], 3)
     pending.extend(w_plane(k).wait_send for k in (1, 2, 3))
 
     def finish_row(r):
         att_copy(r).wait_send()
-        fine_copy(r).wait()
 
     pending.append(lambda: loop(0, 4, finish_row))
 
@@ -448,8 +413,6 @@
     w_core.start()
     pending.append(w_core.wait_send)
     pending.append(lambda: loop(1, 16, lambda k: g_copy(k).wait_send()))
-    for r in range(4):
-        fine_copy(r).start()
 
     prow = iota((256, 256), 0)
     plane_ = iota((256, 256), 1)
@@ -482,7 +445,7 @@
         kvs[g] = jnp.where(half, kv * (lax.rsqrt(mean + EPSILON) * 0.125), kv).astype(BF)
         query = qkv[:, 128:]
         mean = jnp.sum(query * query, axis=-1, keepdims=True) * (1.0 / 64.0)
-        scale = coarse_scales[z + 8 * g] * (LOG2E / 8.0)
+        scale = coarse_scales[2 * z + g] * (LOG2E / 8.0)
         qsend[g] = (query * (lax.rsqrt(mean + EPSILON) * scale)).astype(BF)
 
     def q_copy(k):
@@ -555,43 +518,64 @@
                 start = ((hi * 2 + cc) * 8 + zz) * 16
                 ob[hi, zz, 16 * cc : 16 * cc + 16] = result[start : start + 16]
 
+    owner_c = lax.div(z, 4)
+
     def r_copy(k):
         to_z = lax.rem(z + lax.div(k, 2), 8)
         to_xh = lax.rem(xh + lax.rem(k, 2), 2)
+        slot = 2 * lax.rem(z, 4) + c
         return remote(
             ob.at[to_xh, to_z],
-            rb.at[z, xh],
+            rb.at[slot, xh],
             r_send.at[k],
-            r_recv.at[k],
-            dev(to_z, y, 2 * to_xh + c, core),
-        )
-
-    def r_from(k):
-        from_z = lax.rem(z + 8 - lax.div(k, 2), 8)
-        from_xh = lax.rem(xh + lax.rem(k, 2), 2)
-        return remote(
-            ob.at[from_xh, from_z],
-            rb.at[from_z, from_xh],
-            r_send.at[k],
-            r_recv.at[k],
-            dev(from_z, y, 2 * from_xh + c, core),
-        )
-
-    loop(1, 16, lambda k: r_copy(k).start())
-    pending.append(lambda: loop(1, 16, lambda k: r_copy(k).wait_send()))
-    rb[z, xh] = ob[xh, z]
-    loop(1, 16, lambda k: r_from(k).wait_recv())
+            r_recv.at[2 * slot + xh],
+            dev(to_z, y, 2 * to_xh + owner_c, core),
+        )
+
+    mine = owner_c == c
+
+    @pl.when(jnp.logical_not(mine))
+    def _():
+        r_copy(0).start()
+
+    for k in (8, 9, 7, 11, 6, 10, 5, 13, 4, 12, 3, 15, 2, 14, 1):
+        r_copy(k).start()
+
+    @pl.when(mine)
+    def _():
+        rb[2 * lax.rem(z, 4) + c, xh] = ob[xh, z]
+
+    own_slot = jnp.where(mine, 2 * (2 * lax.rem(z, 4) + c) + xh, -1)
+
+    def r_wait(s):
+        @pl.when(s != own_slot)
+        def _():
+            remote(
+                ob.at[0, 0],
+                rb.at[lax.div(s, 2), lax.rem(s, 2)],
+                r_send.at[0],
+                r_recv.at[s],
+                partner,
+            ).wait_recv()
+
+    loop(0, 16, r_wait)
+
+    def finish_returns():
+        @pl.when(jnp.logical_not(mine))
+        def _():
+            r_copy(0).wait_send()
+
+        loop(1, 16, lambda k: r_copy(k).wait_send())
+
+    pending.append(finish_returns)
     half3 = iota((32, 128), 1) < 64
     for p in range(4):
         even = rb[2 * p, 0].astype(F32) + rb[2 * p, 1].astype(F32)
         odd = rb[2 * p + 1, 0].astype(F32) + rb[2 * p + 1, 1].astype(F32)
         upper = jnp.where(half3, pltpu.roll(even, 64, 1), odd)
         lower = jnp.where(half3, even, pltpu.roll(odd, 64, 1))
-        cv_v[:, 128 * p : 128 * p + 128] = (upper / lower).astype(BF)
-    cv_copy = pltpu.make_async_copy(cv_v, coarse_out.at[0], load_sem.at[0])
-    cv_copy.start()
-
-    pending.append(cv_copy.wait)
+        coarse_out[0, :, 128 * p : 128 * p + 128] = (upper / lower).astype(BF)
+
     for wait in pending:
         wait()
 
@@ -617,11 +601,11 @@
     return pl.pallas_call(
         kernel,
         out_shape=(
-            jax.ShapeDtypeStruct((4, 128, 256), BF),
-            jax.ShapeDtypeStruct((1, 32, 512), BF),
+            pltpu.VMEM((4, 128, 256), BF),
+            pltpu.VMEM((1, 32, 512), BF),
         ),
         in_specs=[hbm] * 12,
-        out_specs=(hbm, hbm),
+        out_specs=(pl.BlockSpec(memory_space=vmem),) * 2,
         scratch_shapes=[
             vmem((10, 128, 512), BF),
             vmem((1000, 256), BF),
@@ -637,11 +621,9 @@
             vmem((10, 128, 256), BF),
             vmem((4, 128, 256), BF),
             vmem((4, 128, 256), BF),
-            vmem((4, 128, 256), BF),
             vmem((2, 16, 512), BF),
             vmem((8, 2, 16, 512), BF),
             vmem((2, 8, 512), F32),
-            vmem((32, 512), BF),
             vmem((2, 4, 4, 32, 512), BF),
             vmem((2, 128, 128), BF),
             vmem((2, 128, 128), BF),
@@ -651,7 +633,6 @@
             vmem((512, 128), F32),
             vmem((2, 8, 32, 128), BF),
             vmem((8, 2, 32, 128), BF),
-            vmem((32, 512), BF),
             smem((1,), jnp.int32),
             smem((1,), jnp.int32),
             smem((8,), F32),
@@ -680,7 +661,7 @@
             dma((16,)),
         ],
         compiler_params=pltpu.CompilerParams(
-            collective_id=0, has_side_effects=True, vmem_limit_bytes=62 * 1024 * 1024
+            collective_id=0, has_side_effects=True, vmem_limit_bytes=56 * 1024 * 1024
         ),
     )(
         timestep,

time: 60.4 us -> 55.1 us (0.912); the launches traced: 59.6 us -> 54.9 us
  Pallas kernels: 54.6 us -> 51.7 us
  local copies, waits for them, and re-layouts: 3.04 us -> 1.32 us
    pallas_call x1, Pallas kernels: 54.6 us -> 51.7 us  [shards(): pl.pallas_call(kernel, out_shape=(pltpu.VMEM((4, 128, 256), BF), pltpu.VM...]
    unnamed x2, local copies, waits for them, and re-layouts: 3.04 us -> 1.32 us
where the time goes in v3:
time: 55.1 us; the launch traced here: 54.9 us
  Pallas kernels  51.7 us (94%)
  between operations  1.93 us (4%)
  local copies, waits for them, and re-layouts  1.32 us (2%)
    pallas_call x1, Pallas kernels, shards(): pl.pallas_call(kernel, out_shape=(pltpu.VMEM((4, 128, 256), BF), pltpu.VM...  51.7 us
    unnamed x2, local copies, waits for them, and re-layouts  1.32 us

profile of v3, /device:TPU:1, one launch (start us, length us, event | category | flops | bytes accessed | tf_op | source)
XLA Modules:
  0.0 54.9 jit_solution(17800832163097488207)
XLA Ops:
  1.9 51.7 %shard_map.131 = (bf16[4,128,256]{2,1,0:T(8,128)(2,1)S(1)}, bf16[1,32,512]{2,1,0:T(8,128)(2,1)S(1)}) custom-call(s32[1]{0:T(128)S(6)} %copy.18.timestep_h, s32[1]{0:T(128)S(6)} %copy.19.label_h, f32[8]{0:T(128)} %fine_scales_h.1, f32[16]{0:T(128)} %coarse_scales_h.1, bf16[4,128,512]{2,1,0:T(8,128)(2,1)} %image.1, bf16[1000,256]{1,0:T(8,128)(2,1)} %class_table.1, ...), custom_call_target="tpu_custom_call" | custom-call | tf_op jit(solution)/shard_map/pallas_call | solution.py:601
  53.6 0.7 %copy.16 = bf16[4,128,256]{2,1,0:T(8,128)(2,1)} copy(bf16[4,128,256]{2,1,0:T(8,128)(2,1)S(1)} %get-tuple-element.2) | data formatting | bytes 524288
  54.3 0.6 %copy.17 = bf16[1,32,512]{2,1,0:T(8,128)(2,1)} copy(bf16[1,32,512]{2,1,0:T(8,128)(2,1)S(1)} %get-tuple-element.3) | data formatting | bytes 65536

commit v4 on v3

--- a/solution.py
+++ b/solution.py
@@ -13,6 +13,7 @@
 F32 = jnp.float32
 MESH = pl.DeviceIdType.MESH
 BANDS = 128
+ORDER = (0, 1, 7, 2, 6, 3, 5, 4)
 
 
 def dot(a, b):
@@ -65,7 +66,6 @@
     kvb,
     qb,
     num,
-    den,
     ob,
     rb,
     timestep,
@@ -360,6 +360,8 @@
     attend_row(0)
     pl.semaphore_wait(entered.at[0], 6)
     vouch(1, [near(2, 0, 0), near(-2, 0, 0), near(0, 2, 0)])
+    for k in (2, 1, 3):
+        w_line(k).start()
     loads[5].wait()
     fout_copy.wait_recv()
     fout_pass.start()
@@ -368,16 +370,14 @@
     attend_row(1)
     pl.semaphore_wait(entered.at[1], 3)
     vouch(2, [near(0, 0, 1), near(0, 0, -1), near(0, 0, 2)])
-    for k in (2, 1, 3):
-        w_line(k).start()
     new_row(2)
     attend_row(2)
-    new_row(3)
-    attend_row(3)
     for k in (1, 2, 3):
         w_line(k).wait_recv()
     for k in (2, 1, 3):
         w_plane(k).start()
+    new_row(3)
+    attend_row(3)
     fout_pass.wait_recv()
     for copy in merges:
         copy.wait()
@@ -396,23 +396,39 @@
 
     mg[0] = merged[0:16]
     mg[1] = merged[16:32]
-    gb[z, c] = mg[c]
+    gb[0, c] = mg[c]
 
     def g_copy(k):
-        to_z = lax.rem(z + lax.div(k, 2), 8)
-        to_c = lax.rem(c + lax.rem(k, 2), 2)
+        to_z = lax.rem(z + k // 2, 8)
+        to_c = lax.rem(c + k % 2, 2)
         return remote(
-            mg.at[to_c], gb.at[z, c], g_send.at[k], g_recv.at[k], dev(to_z, y, 2 * xh + to_c, core)
-        )
-
-    loop(1, 16, lambda k: g_copy(k).start())
+            mg.at[to_c],
+            gb.at[ORDER.index(k // 2), c],
+            g_send.at[k],
+            g_recv.at[k],
+            dev(to_z, y, 2 * xh + to_c, core),
+        )
+
+    def g_wait(k):
+        from_c = lax.rem(c + k % 2, 2)
+        remote(
+            mg.at[0],
+            gb.at[ORDER.index(k // 2), from_c],
+            g_send.at[k],
+            g_recv.at[k],
+            partner,
+        ).wait_recv()
+
+    sent = [2 * d + e for d in ORDER for e in range(2) if d + e > 0]
+    for k in sent:
+        g_copy(k).start()
     for k in (1, 2, 3):
         w_plane(k).wait_recv()
     for k in (1, 2, 3):
         w_line(k).wait_send()
     w_core.start()
     pending.append(w_core.wait_send)
-    pending.append(lambda: loop(1, 16, lambda k: g_copy(k).wait_send()))
+    pending.extend(g_copy(k).wait_send for k in sent)
 
     prow = iota((256, 256), 0)
     plane_ = iota((256, 256), 1)
@@ -420,33 +436,40 @@
     column = 24 * lax.div(prow, 32) + inner
     target = jnp.where(plane_ < 128, plane_ + 64, jnp.where(plane_ < 192, plane_ - 128, -1))
     select = ((inner < 24) & (column == target)).astype(F32).astype(BF)
-    half = iota((128, 128), 1) < 64
+    half = iota((64, 128), 1) < 64
 
     gain_copy.wait_recv()
     w_core.wait_recv()
-    loop(1, 16, lambda k: g_copy(k).wait_recv())
-    x0 = gb[:, 0].reshape(128, 512).astype(F32)
-    x1 = gb[:, 1].reshape(128, 512).astype(F32)
-    square = jnp.sum(x0 * x0, axis=-1, keepdims=True) + jnp.sum(x1 * x1, axis=-1, keepdims=True)
-    factor = lax.rsqrt(square * (1.0 / 1024.0) + EPSILON)
-    s0 = (x0 * gain_v[0, 0:1, :]).astype(BF)
-    s1 = (x1 * gain_v[1, 0:1, :]).astype(BF)
-    for g in range(2):
-        weights = [
-            jnp.concatenate(
-                [wb[j % 2, 2 * g + j // 4, 2 * ((j // 2) % 2) + cc] for j in range(8)], axis=0
-            )
-            for cc in range(2)
-        ]
-        qkv = (dot_t(s0, weights[0]) + dot_t(s1, weights[1])) * factor
-        qkv = dot(qkv.astype(BF), select)
-        kv = qkv[:, :128]
-        mean = jnp.sum(jnp.where(half, kv * kv, 0.0), axis=-1, keepdims=True) * (1.0 / 64.0)
-        kvs[g] = jnp.where(half, kv * (lax.rsqrt(mean + EPSILON) * 0.125), kv).astype(BF)
-        query = qkv[:, 128:]
-        mean = jnp.sum(query * query, axis=-1, keepdims=True) * (1.0 / 64.0)
-        scale = coarse_scales[2 * z + g] * (LOG2E / 8.0)
-        qsend[g] = (query * (lax.rsqrt(mean + EPSILON) * scale)).astype(BF)
+
+    def project(part):
+        for k in sent[:7] if part == 0 else sent[7:]:
+            g_wait(k)
+        x0 = gb[4 * part : 4 * part + 4, 0].reshape(64, 512).astype(F32)
+        x1 = gb[4 * part : 4 * part + 4, 1].reshape(64, 512).astype(F32)
+        square = jnp.sum(x0 * x0, axis=-1, keepdims=True) + jnp.sum(
+            x1 * x1, axis=-1, keepdims=True
+        )
+        factor = lax.rsqrt(square * (1.0 / 1024.0) + EPSILON)
+        s0 = (x0 * gain_v[0, 0:1, :]).astype(BF)
+        s1 = (x1 * gain_v[1, 0:1, :]).astype(BF)
+        for g in range(2):
+            weights = [
+                jnp.concatenate(
+                    [wb[j % 2, 2 * g + j // 4, 2 * ((j // 2) % 2) + cc] for j in range(8)], axis=0
+                )
+                for cc in range(2)
+            ]
+            qkv = (dot_t(s0, weights[0]) + dot_t(s1, weights[1])) * factor
+            qkv = dot(qkv.astype(BF), select)
+            kv = qkv[:, :128]
+            mean = jnp.sum(jnp.where(half, kv * kv, 0.0), axis=-1, keepdims=True) * (1.0 / 64.0)
+            kvs[part, g] = jnp.where(half, kv * (lax.rsqrt(mean + EPSILON) * 0.125), kv).astype(BF)
+            query = qkv[:, 128:]
+            mean = jnp.sum(query * query, axis=-1, keepdims=True) * (1.0 / 64.0)
+            scale = coarse_scales[2 * z + g] * (LOG2E / 8.0)
+            qsend[g, 64 * part : 64 * part + 64] = (
+                query * (lax.rsqrt(mean + EPSILON) * scale)
+            ).astype(BF)
 
     def q_copy(k):
         to_xh = lax.rem(xh + lax.div(k, 2), 2)
@@ -459,59 +482,73 @@
             dev(z, y, 2 * to_xh + to_c, core),
         )
 
-    def kv_copy(k):
-        to_y = lax.rem(y + lax.div(k, 2), 4)
-        to_c = lax.rem(c + lax.rem(k, 2), 2)
+    def kv_copy(part, k):
+        to_y = lax.rem(y + k // 2, 4)
+        to_c = lax.rem(c + k % 2, 2)
         return remote(
-            kvs.at[to_c],
-            kvb.at[core, y, c],
-            kv_send.at[k],
-            kv_recv.at[k],
+            kvs.at[part, to_c],
+            kvb.at[part, core, y, c],
+            kv_send.at[8 * part + k],
+            kv_recv.at[8 * part + k],
             dev(z, to_y, 2 * xh + to_c, core),
         )
 
-    def forward(k):
+    def kv_wait(part, k):
+        remote(
+            kvs.at[part, 0],
+            kvb.at[part, core, lax.rem(y + 4 - k // 2, 4), lax.rem(c + k % 2, 2)],
+            kv_send.at[8 * part + k],
+            kv_recv.at[8 * part + k],
+            partner,
+        ).wait_recv()
+
+    def forward(part, k):
         from_y = lax.rem(y + 4 - k, 4)
         return remote(
-            kvb.at[core, from_y], kvb.at[core, from_y], fw_send.at[k], fw_recv.at[k], sibling
-        )
-
-    for k in (4, 5, 2, 3, 6, 7, 1):
-        kv_copy(k).start()
+            kvb.at[part, core, from_y],
+            kvb.at[part, core, from_y],
+            fw_send.at[4 * part + k],
+            fw_recv.at[4 * part + k],
+            sibling,
+        )
+
+    for part in range(2):
+        project(part)
+        for k in (4, 5, 2, 3, 6, 7, 1):
+            kv_copy(part, k).start()
+            pending.append(kv_copy(part, k).wait_send)
+        kvb[part, core, y, c] = kvs[part, c]
     loop(1, 4, lambda k: q_copy(k).start())
     pending.append(lambda: loop(1, 4, lambda k: q_copy(k).wait_send()))
-    pending.append(lambda: loop(1, 8, lambda k: kv_copy(k).wait_send()))
-    kvb[core, y, c] = kvs[c]
     qb[xh, c] = qsend[c]
     num[...] = jnp.zeros_like(num)
-    den[...] = jnp.zeros_like(den)
+    half4 = iota((512, 128), 1) < 64
+
+    def attend(part, which):
+        block = kvb[part, which].reshape(512, 128)
+        weight = jnp.exp2(dot_t(qb[...].reshape(512, 128), block)).astype(BF)
+        num[...] += dot(weight, jnp.where(half4, 1.0, block.astype(F32)).astype(BF))
+
+    def pass_on(part):
+        for k in (1, 3, 2, 0):
+            if k > 0:
+                kv_wait(part, 2 * k)
+            kv_wait(part, 2 * k + 1)
+            forward(part, k).start()
+            pending.append(forward(part, k).wait_send)
+
+    pass_on(0)
+    pass_on(1)
     loop(1, 4, lambda k: q_copy(k).wait_recv())
-
-    def attend(which, from_y):
-        block = kvb[which, from_y].reshape(256, 128)
-        weight = jnp.exp2(dot_t(qb[...].reshape(512, 128), block))
-        den[...] += weight[:, :128] + weight[:, 128:]
-        num[...] += dot(weight.astype(BF), block)
-
-    def direct(k):
-        @pl.when(k > 0)
-        def _():
-            kv_copy(2 * k).wait_recv()
-
-        kv_copy(2 * k + 1).wait_recv()
-        forward(k).start()
-        attend(core, lax.rem(y + 4 - k, 4))
-
-    def forwarded(k):
-        forward(k).wait_recv()
-        attend(1 - core, lax.rem(y + 4 - k, 4))
-
-    loop(0, 4, direct)
-    loop(0, 4, forwarded)
-    pending.append(lambda: loop(0, 4, lambda k: forward(k).wait_send()))
-
-    half2 = iota((512, 128), 1) < 64
-    result = jnp.where(half2, jnp.sum(den[...], axis=-1, keepdims=True), num[...]).astype(BF)
+    attend(0, core)
+    attend(1, core)
+    for k in range(4):
+        forward(0, k).wait_recv()
+    attend(0, 1 - core)
+    for k in range(4):
+        forward(1, k).wait_recv()
+    attend(1, 1 - core)
+    result = num[...].astype(BF)
     for hi in range(2):
         for cc in range(2):
             for zz in range(8):
@@ -521,11 +558,11 @@
     owner_c = lax.div(z, 4)
 
     def r_copy(k):
-        to_z = lax.rem(z + lax.div(k, 2), 8)
-        to_xh = lax.rem(xh + lax.rem(k, 2), 2)
+        to_z = lax.rem(z + k // 2, 8)
+        to_xh = lax.rem(xh + k % 2, 2)
         slot = 2 * lax.rem(z, 4) + c
         return remote(
-            ob.at[to_xh, to_z],
+            ob.at[to_xh, ORDER.index((8 - k // 2) % 8)],
             rb.at[slot, xh],
             r_send.at[k],
             r_recv.at[2 * slot + xh],
@@ -543,7 +580,7 @@
 
     @pl.when(mine)
     def _():
-        rb[2 * lax.rem(z, 4) + c, xh] = ob[xh, z]
+        rb[2 * lax.rem(z, 4) + c, xh] = ob[xh, 0]
 
     own_slot = jnp.where(mine, 2 * (2 * lax.rem(z, 4) + c) + xh, -1)
 
@@ -565,7 +602,8 @@
         def _():
             r_copy(0).wait_send()
 
-        loop(1, 16, lambda k: r_copy(k).wait_send())
+        for k in range(1, 16):
+            r_copy(k).wait_send()
 
     pending.append(finish_returns)
     half3 = iota((32, 128), 1) < 64
@@ -625,11 +663,10 @@
             vmem((8, 2, 16, 512), BF),
             vmem((2, 8, 512), F32),
             vmem((2, 4, 4, 32, 512), BF),
+            vmem((2, 2, 64, 128), BF),
             vmem((2, 128, 128), BF),
-            vmem((2, 128, 128), BF),
-            vmem((2, 4, 2, 128, 128), BF),
+            vmem((2, 2, 4, 2, 64, 128), BF),
             vmem((2, 2, 128, 128), BF),
-            vmem((512, 128), F32),
             vmem((512, 128), F32),
             vmem((2, 8, 32, 128), BF),
             vmem((8, 2, 32, 128), BF),
@@ -651,12 +688,12 @@
             dma((8,)),
             dma((16,)),
             dma((16,)),
+            dma((16,)),
+            dma((16,)),
+            dma((4,)),
+            dma((4,)),
             dma((8,)),
             dma((8,)),
-            dma((4,)),
-            dma((4,)),
-            dma((4,)),
-            dma((4,)),
             dma((16,)),
             dma((16,)),
         ],

time: 55.1 us -> 53.8 us (0.976)
  Pallas kernels: 51.7 us -> 50.2 us
    pallas_call x1, Pallas kernels: 51.7 us -> 50.2 us  [shards(): pl.pallas_call(kernel, out_shape=(pltpu.VMEM((4, 128, 256), BF), pltpu.VM...]
where the time goes in v4:
time: 53.8 us; the launch traced here: 53.4 us
  Pallas kernels  50.2 us (93%)
  between operations  1.93 us (4%)
  local copies, waits for them, and re-layouts  1.32 us (2%)
    pallas_call x1, Pallas kernels, shards(): pl.pallas_call(kernel, out_shape=(pltpu.VMEM((4, 128, 256), BF), pltpu.VM...  50.2 us
    unnamed x2, local copies, waits for them, and re-layouts  1.32 us

profile of v4, /device:TPU:1, one launch (start us, length us, event | category | flops | bytes accessed | tf_op | source)
XLA Modules:
  0.0 53.4 jit_solution(6228151124840245027)
XLA Ops:
  1.9 50.2 %shard_map.131 = (bf16[4,128,256]{2,1,0:T(8,128)(2,1)S(1)}, bf16[1,32,512]{2,1,0:T(8,128)(2,1)S(1)}) custom-call(s32[1]{0:T(128)S(6)} %copy.18.timestep_h, s32[1]{0:T(128)S(6)} %copy.19.label_h, f32[8]{0:T(128)} %fine_scales_h.1, f32[16]{0:T(128)} %coarse_scales_h.1, bf16[4,128,512]{2,1,0:T(8,128)(2,1)} %image.1, bf16[1000,256]{1,0:T(8,128)(2,1)} %class_table.1, ...), custom_call_target="tpu_custom_call" | custom-call | tf_op jit(solution)/shard_map/pallas_call | solution.py:639
  52.1 0.7 %copy.16 = bf16[4,128,256]{2,1,0:T(8,128)(2,1)} copy(bf16[4,128,256]{2,1,0:T(8,128)(2,1)S(1)} %get-tuple-element.2) | data formatting | bytes 524288
  52.8 0.6 %copy.17 = bf16[1,32,512]{2,1,0:T(8,128)(2,1)} copy(bf16[1,32,512]{2,1,0:T(8,128)(2,1)S(1)} %get-tuple-element.3) | data formatting | bytes 65536

commit v5 on v4

--- a/solution.py
+++ b/solution.py
@@ -61,6 +61,7 @@
     gb,
     gain_v,
     wb,
+    wsel,
     kvs,
     qsend,
     kvb,
@@ -430,8 +431,8 @@
     pending.append(w_core.wait_send)
     pending.extend(g_copy(k).wait_send for k in sent)
 
-    prow = iota((256, 256), 0)
-    plane_ = iota((256, 256), 1)
+    prow = iota((256, 256), 1)
+    plane_ = iota((256, 256), 0)
     inner = lax.rem(prow, 32)
     column = 24 * lax.div(prow, 32) + inner
     target = jnp.where(plane_ < 128, plane_ + 64, jnp.where(plane_ < 192, plane_ - 128, -1))
@@ -440,6 +441,10 @@
 
     gain_copy.wait_recv()
     w_core.wait_recv()
+    for g in range(2):
+        for cc in range(2):
+            blocks = [wb[j % 2, 2 * g + j // 4, 2 * ((j // 2) % 2) + cc] for j in range(8)]
+            wsel[g, cc] = dot(select, jnp.concatenate(blocks, axis=0)).astype(BF)
 
     def project(part):
         for k in sent[:7] if part == 0 else sent[7:]:
@@ -453,14 +458,8 @@
         s0 = (x0 * gain_v[0, 0:1, :]).astype(BF)
         s1 = (x1 * gain_v[1, 0:1, :]).astype(BF)
         for g in range(2):
-            weights = [
-                jnp.concatenate(
-                    [wb[j % 2, 2 * g + j // 4, 2 * ((j // 2) % 2) + cc] for j in range(8)], axis=0
-                )
-                for cc in range(2)
-            ]
-            qkv = (dot_t(s0, weights[0]) + dot_t(s1, weights[1])) * factor
-            qkv = dot(qkv.astype(BF), select)
+            qkv = (dot_t(s0, wsel[g, 0]) + dot_t(s1, wsel[g, 1])) * factor
+            qkv = qkv.astype(BF).astype(F32)
             kv = qkv[:, :128]
             mean = jnp.sum(jnp.where(half, kv * kv, 0.0), axis=-1, keepdims=True) * (1.0 / 64.0)
             kvs[part, g] = jnp.where(half, kv * (lax.rsqrt(mean + EPSILON) * 0.125), kv).astype(BF)
@@ -595,7 +594,6 @@
                 partner,
             ).wait_recv()
 
-    loop(0, 16, r_wait)
 
     def finish_returns():
         @pl.when(jnp.logical_not(mine))
@@ -606,6 +604,9 @@
             r_copy(k).wait_send()
 
     pending.append(finish_returns)
+    for wait in pending:
+        wait()
+    loop(0, 16, r_wait)
     half3 = iota((32, 128), 1) < 64
     for p in range(4):
         even = rb[2 * p, 0].astype(F32) + rb[2 * p, 1].astype(F32)
@@ -613,9 +614,6 @@
         upper = jnp.where(half3, pltpu.roll(even, 64, 1), odd)
         lower = jnp.where(half3, even, pltpu.roll(odd, 64, 1))
         coarse_out[0, :, 128 * p : 128 * p + 128] = (upper / lower).astype(BF)
-
-    for wait in pending:
-        wait()
 
 
 def shards(
@@ -663,6 +661,7 @@
             vmem((8, 2, 16, 512), BF),
             vmem((2, 8, 512), F32),
             vmem((2, 4, 4, 32, 512), BF),
+            vmem((2, 2, 256, 512), BF),
             vmem((2, 2, 64, 128), BF),
             vmem((2, 128, 128), BF),
             vmem((2, 2, 4, 2, 64, 128), BF),

time: 53.8 us -> 53.3 us (level)
  no operation moved by 1% of the time
where the time goes in v5:
time: 53.3 us; the launch traced here: 53.2 us
  Pallas kernels  49.9 us (94%)
  between operations  1.93 us (4%)
  local copies, waits for them, and re-layouts  1.32 us (2%)
    pallas_call x1, Pallas kernels, shards(): pl.pallas_call(kernel, out_shape=(pltpu.VMEM((4, 128, 256), BF), pltpu.VM...  49.9 us
    unnamed x2, local copies, waits for them, and re-layouts  1.32 us

profile of v5, /device:TPU:1, one launch (start us, length us, event | category | flops | bytes accessed | tf_op | source)
XLA Modules:
  0.0 53.2 jit_solution(15980866034185714531)
XLA Ops:
  1.9 49.9 %shard_map.131 = (bf16[4,128,256]{2,1,0:T(8,128)(2,1)S(1)}, bf16[1,32,512]{2,1,0:T(8,128)(2,1)S(1)}) custom-call(s32[1]{0:T(128)S(6)} %copy.18.timestep_h, s32[1]{0:T(128)S(6)} %copy.19.label_h, f32[8]{0:T(128)} %fine_scales_h.1, f32[16]{0:T(128)} %coarse_scales_h.1, bf16[4,128,512]{2,1,0:T(8,128)(2,1)} %image.1, bf16[1000,256]{1,0:T(8,128)(2,1)} %class_table.1, ...), custom_call_target="tpu_custom_call" | custom-call | tf_op jit(solution)/shard_map/pallas_call | solution.py:637
  51.8 0.7 %copy.16 = bf16[4,128,256]{2,1,0:T(8,128)(2,1)} copy(bf16[4,128,256]{2,1,0:T(8,128)(2,1)S(1)} %get-tuple-element.2) | data formatting | bytes 524288
  52.5 0.6 %copy.17 = bf16[1,32,512]{2,1,0:T(8,128)(2,1)} copy(bf16[1,32,512]{2,1,0:T(8,128)(2,1)S(1)} %get-tuple-element.3) | data formatting | bytes 65536

commit v6 on v5

--- a/solution.py
+++ b/solution.py
@@ -377,14 +377,17 @@
         w_line(k).wait_recv()
     for k in (2, 1, 3):
         w_plane(k).start()
+    fout_pass.wait_recv()
+    merges[0].wait()
+    att_copy(0).wait_recv()
+    merged = mix_row(0)
     new_row(3)
     attend_row(3)
-    fout_pass.wait_recv()
-    for copy in merges:
-        copy.wait()
-    for r in range(3):
+    for r in (1, 2):
+        merges[r].wait()
         att_copy(r).wait_recv()
-    merged = mix_row(0) + mix_row(1) + mix_row(2)
+    merges[3].wait()
+    merged = merged + (mix_row(1) + mix_row(2))
     att_copy(3).wait_recv()
     merged = (merged + mix_row(3)).astype(BF)
     pl.semaphore_wait(entered.at[2], 3)

time: 53.3 us -> 53.2 us (level)
  no operation moved by 1% of the time
where the time goes in v6:
time: 53.2 us; the launch traced here: 52.9 us
  Pallas kernels  49.6 us (93%)
  between operations  1.93 us (4%)
  local copies, waits for them, and re-layouts  1.32 us (2%)
    pallas_call x1, Pallas kernels, shards(): pl.pallas_call(kernel, out_shape=(pltpu.VMEM((4, 128, 256), BF), pltpu.VM...  49.6 us
    unnamed x2, local copies, waits for them, and re-layouts  1.32 us

profile of v6, /device:TPU:1, one launch (start us, length us, event | category | flops | bytes accessed | tf_op | source)
XLA Modules:
  0.0 52.9 jit_solution(5741743593693493022)
XLA Ops:
  1.9 49.6 %shard_map.131 = (bf16[4,128,256]{2,1,0:T(8,128)(2,1)S(1)}, bf16[1,32,512]{2,1,0:T(8,128)(2,1)S(1)}) custom-call(s32[1]{0:T(128)S(6)} %copy.18.timestep_h, s32[1]{0:T(128)S(6)} %copy.19.label_h, f32[8]{0:T(128)} %fine_scales_h.1, f32[16]{0:T(128)} %coarse_scales_h.1, bf16[4,128,512]{2,1,0:T(8,128)(2,1)} %image.1, bf16[1000,256]{1,0:T(8,128)(2,1)} %class_table.1, ...), custom_call_target="tpu_custom_call" | custom-call | tf_op jit(solution)/shard_map/pallas_call | solution.py:640
  51.6 0.7 %copy.16 = bf16[4,128,256]{2,1,0:T(8,128)(2,1)} copy(bf16[4,128,256]{2,1,0:T(8,128)(2,1)S(1)} %get-tuple-element.2) | data formatting | bytes 524288
  52.3 0.6 %copy.17 = bf16[1,32,512]{2,1,0:T(8,128)(2,1)} copy(bf16[1,32,512]{2,1,0:T(8,128)(2,1)S(1)} %get-tuple-element.3) | data formatting | bytes 65536
